TPU v7x, 512 devices: a whole 4x8x8 slice. The times are simulated.
512 devices in a mesh: blk: 16 (over y_lo, x), grp: 32 (over y_hi, z, core).
Axes of the slice: x: 4, y: 8 (y_hi: 2, y_lo: 4; y = y_hi * 4 + y_lo), z: 8, core: 2. Of those that a mesh axis runs over, the one named last changes fastest.
Arguments:
- tower_images: bfloat16 [32768, 1152], P(('blk', 'grp')), may hold values from -0.17675781 to 0.17675781
- owners: int32 [32768], P(('blk', 'grp')), may hold values from 0 to 895, as said below
- counts: int32 [512], P(('blk', 'grp')), may hold values from 1 to 64, as said below
- text: bfloat16 [14336, 1152], P(('blk', 'grp')), may hold values from -0.17675781 to 0.17675781
- logit_scale: float32 [1], replicated, may hold values from 8 to 12
- logit_bias: float32 [1], replicated, may hold values from -6 to -3
Outputs:
- image_grad: float32 [32768, 1152], P(('blk', 'grp'))
- text_grad: float32 [14336, 1152], P(('blk', 'grp'))
Inputs may be any that keep to these rules, and one draw needn't show every extreme that they name: `owners`: tower devices come in data groups of 32 consecutive devices. In each group the first counts[u] slots of tower u name pairs of that group, and every one of the group's 32 * 28 pairs is named by exactly one live slot; a pair index q belongs to owner device q // 28 of the group. At most 2 live slots of one tower name pairs of one owner, and some tower reaches 2 in every group. Slots past the count hold arbitrary indices in range. `counts`: live slots of a tower device; over a data group they sum to 896, and 64 is reached in every group.
All inputs are finite; a program needn't handle non-finite values.
Results may differ from a plain program's by a relative error of at most 0.005.
Values may be sent and summed in bfloat16 or wider, within the bound.
A program may use at most 64 MiB of HBM per device.

v0:
```python
import jax
import jax.numpy as jnp
from jax import lax
from jax.sharding import PartitionSpec as P


def passed_along(block, axis, distance):
    devices = range(lax.axis_size(axis))
    route = [((i - distance) % len(devices), i) for i in devices]
    return lax.ppermute(block, axis, route)


def unit_rows(values):
    wide = values.astype(jnp.float32)
    inverse = lax.rsqrt(jnp.sum(wide * wide, axis=-1, keepdims=True) + 1e-06)
    return (wide * inverse, inverse)


def unit_back(grad, unit, inverse):
    return (grad - unit * jnp.sum(unit * grad, axis=-1, keepdims=True)) * inverse


def pass_images(images_here):
    return passed_along(images_here, "blk", 1)


def routing(owner_list, live_count, pairs, groups):
    live = jnp.arange(owner_list.shape[0], dtype=jnp.int32) < live_count
    target = owner_list // pairs
    row = owner_list % pairs
    onehot = (
        (target[:, None] == jnp.arange(groups, dtype=jnp.int32)[None, :]) & live[:, None]
    ).astype(jnp.int32)
    before = jnp.cumsum(onehot, axis=0) - onehot
    rank = jnp.sum(before * onehot, axis=1)
    return (target, row, rank, live)


def shards(tower_images, owners, counts, text, logit_scale, logit_bias):
    cap = tower_images.shape[0]
    width = tower_images.shape[1]
    pairs = text.shape[0]
    groups = lax.axis_size("grp")
    blocks = lax.axis_size("blk")
    light_count = groups - groups // 4
    per_owner = max(2, (pairs - groups // 2 + light_count - 1) // light_count)
    lanes = groups * per_owner
    my_member = lax.axis_index("grp")
    target, row, rank, live = routing(owners, counts[0], pairs, groups)
    slot_index = jnp.where(live, target * per_owner + rank, -1)
    chooser = (slot_index[None, :] == jnp.arange(lanes, dtype=jnp.int32)[:, None]).astype(
        jnp.float32
    )
    all_owners, all_counts = (
        lax.all_gather(owners, "grp", axis=0, tiled=True),
        lax.all_gather(counts, "grp", axis=0, tiled=True),
    )
    table = all_owners.reshape(groups, cap)
    t_target, t_row, t_rank, t_live = jax.vmap(routing, in_axes=(0, 0, None, None))(
        table, all_counts, pairs, groups
    )
    mine = (t_live & (t_target == my_member)).reshape(-1)
    position = (jnp.arange(groups, dtype=jnp.int32)[:, None] * per_owner + t_rank).reshape(-1)
    row_pick = (
        (t_row.reshape(-1)[None, :] == jnp.arange(pairs, dtype=jnp.int32)[:, None]) & mine[None, :]
    ).astype(jnp.float32)
    lane_pick = (position[:, None] == jnp.arange(lanes, dtype=jnp.int32)[None, :]).astype(
        jnp.float32
    )
    placing = jnp.dot(row_pick, lane_pick, precision=lax.Precision.HIGHEST)
    sending = jnp.dot(
        chooser.astype(jnp.bfloat16), tower_images, preferred_element_type=jnp.float32
    ).astype(jnp.bfloat16)
    arrived = lax.all_to_all(
        sending.reshape(groups, per_owner, width), "grp", split_axis=0, concat_axis=0, tiled=True
    )
    own_images = jnp.dot(
        placing.astype(jnp.bfloat16),
        arrived.reshape(lanes, width),
        preferred_element_type=jnp.float32,
    ).astype(jnp.bfloat16)
    image_unit, image_inv = unit_rows(own_images)
    image_low = image_unit.astype(jnp.bfloat16)
    text_unit, text_inv = unit_rows(text)
    group_text = lax.all_gather(text_unit.astype(jnp.bfloat16), "grp", axis=0, tiled=True)
    scale = logit_scale[0]
    bias = logit_bias[0]
    diagonal = (
        jnp.arange(groups * pairs, dtype=jnp.int32)[None, :]
        == (my_member * pairs + jnp.arange(pairs, dtype=jnp.int32))[:, None]
    )

    def stop_terms(images_here, first):
        raw = lax.dot_general(
            images_here, group_text, (((1,), (1,)), ((), ())), preferred_element_type=jnp.float32
        )
        logits = scale * raw + bias
        sign = jnp.where(first & diagonal, 1.0, -1.0).astype(jnp.float32)
        slope = -sign * jax.nn.sigmoid(-sign * logits)
        dscore = (scale * slope).astype(jnp.bfloat16)
        return (jnp.dot(dscore, group_text, preferred_element_type=jnp.float32), dscore)

    seen = jnp.zeros((blocks, pairs, width), jnp.bfloat16)
    scores = jnp.zeros((blocks, pairs, groups * pairs), jnp.bfloat16)
    last_first = jnp.asarray(blocks == 1)

    def visit_travel(stop, carry):
        images_here, carried, seen, scores = carry
        part, dscore = stop_terms(images_here, stop == 0)
        carried = carried + part
        seen = lax.dynamic_update_index_in_dim(seen, images_here, stop, 0)
        scores = lax.dynamic_update_index_in_dim(scores, dscore, stop, 0)
        images_here = pass_images(images_here)
        carried = passed_along(carried, "blk", 1)
        return (images_here, carried, seen, scores)

    carried = jnp.zeros((pairs, width), jnp.float32)
    images_here, carried, seen, scores = lax.fori_loop(
        0, blocks - 1, visit_travel, (image_low, carried, seen, scores)
    )
    part, dscore = stop_terms(images_here, last_first)
    seen = lax.dynamic_update_index_in_dim(seen, images_here, blocks - 1, 0)
    scores = lax.dynamic_update_index_in_dim(scores, dscore, blocks - 1, 0)
    image_unit_grad = passed_along(carried + part, "blk", 1)
    text_terms = lax.dot_general(
        scores, seen, (((0, 1), (0, 1)), ((), ())), preferred_element_type=jnp.float32
    )
    text_unit_grad = lax.psum_scatter(text_terms, "grp", scatter_dimension=0, tiled=True)
    text_grad = unit_back(text_unit_grad, text_unit, text_inv)
    pair_grad = unit_back(image_unit_grad, image_unit, image_inv)
    outgoing = jnp.dot(placing.T, pair_grad, precision=lax.Precision.HIGHEST)
    incoming = lax.all_to_all(
        outgoing.reshape(groups, per_owner, width), "grp", split_axis=0, concat_axis=0, tiled=True
    )
    image_grad = jnp.dot(chooser.T, incoming.reshape(lanes, width), precision=lax.Precision.HIGHEST)
    return (image_grad, text_grad)


def solution(mesh):
    in_specs = (
        P(("blk", "grp"), None),
        P(("blk", "grp")),
        P(("blk", "grp")),
        P(("blk", "grp"), None),
        P(),
        P(),
    )
    out_specs = (P(("blk", "grp"), None), P(("blk", "grp"), None))
    return jax.shard_map(shards, mesh=mesh, in_specs=in_specs, out_specs=out_specs, check_vma=False)
```

profile of v0, /device:TPU:1, one launch (start us, length us, event | category | flops | bytes accessed | tf_op | source)
XLA Modules:
  0.0 512.0 jit_solution(7401901024874922566)
XLA Ops:
  13.2 17.2 %all-to-all-start = ((bf16[32,2,1152]{2,1,0:T(2,128)(2,1)}), bf16[32,2,1152]{2,1,0:T(2,128)(2,1)S(1)}, u32[]{:S(2)}, u32[]{:S(2)}) async-start(bf16[32,2,1152]{2,1,0:T(2,128)(2,1)} %reshape.134), calls=%async_computation | async-start | bytes 294912 | tf_op jit(solution)/shard_map/all_to_all | solution.py:74
  34.0 18.2 %all-reduce.4 = (s32[2048]{0:T(1024)S(1)}, s32[32]{0:T(128)S(1)}) all-reduce(s32[2048]{0:T(1024)S(1)} %dynamic-update-slice, s32[32]{0:T(128)S(1)} %dynamic-update-slice.1), channel_id=1, replica_groups=mesh['blk'=16,'grp'=32] {'grp'}, use_global_device_ids=true, to_apply=%add | all-reduce | flops 2080 | bytes 16640
  58.0 52.4 %all-gather.3.cloned.1.call-done = bf16[32,28,1152]{2,1,0:T(8,128)(2,1)} async-done(((bf16[1,28,1152]{2,1,0:T(8,128)(2,1)}), bf16[32,28,1152]{2,1,0:T(8,128)(2,1)}) %all-gather.3.cloned.1.call-update) | async-done | bytes 2064400 | tf_op jit(solution)/shard_map/all_gather | solution.py:85
  115.1 228.4 %while.20 = (s32[]{:T(128)}, bf16[28,1152]{1,0:T(8,128)(2,1)S(1)}, f32[28,1152]{1,0:T(8,128)S(1)}, bf16[16,28,1152]{2,1,0:T(8,128)(2,1)}, bf16[16,28,896]{2,1,0:...) while((s32[]{:T(128)}, bf16[28,1152]{1,0:T(8,128)(2,1)S(1)}, ...), condition=%wide.region_7.8_spmd.clone, body=%wide.region_6.7_spmd.clone.sunk | while | flops 115963904 | bytes 5652791 | solution.py:118
  115.1 3.0 collective-permute-start
  121.3 3.1 collective-permute-start.1
  125.0 6.9 %collective-permute-done.1 = f32[28,1152]{1,0:T(8,128)S(1)} collective-permute-done((f32[28,1152]{1,0:T(8,128)S(1)}, f32[28,1152]{1,0:T(8,128)S(1)}, u32[]{:S(2)}, u32[]{:S(2)}) %collective-permute-start.1) | collective-permute-done | bytes 129056 | tf_op jit(solution)/shard_map/while/body/eval_jaxpr/ppermute | solution.py:10
  140.9 5.8 %collective-permute-done.1 = f32[28,1152]{1,0:T(8,128)S(1)} collective-permute-done((f32[28,1152]{1,0:T(8,128)S(1)}, f32[28,1152]{1,0:T(8,128)S(1)}, u32[]{:S(2)}, u32[]{:S(2)}) %collective-permute-start.1) | collective-permute-done | bytes 129056 | tf_op jit(solution)/shard_map/while/body/eval_jaxpr/ppermute | solution.py:10
  148.7 2.7 bitcast_dynamic-update-slice_fusion.6
  155.8 5.9 %collective-permute-done.1 = f32[28,1152]{1,0:T(8,128)S(1)} collective-permute-done((f32[28,1152]{1,0:T(8,128)S(1)}, f32[28,1152]{1,0:T(8,128)S(1)}, u32[]{:S(2)}, u32[]{:S(2)}) %collective-permute-start.1) | collective-permute-done | bytes 129056 | tf_op jit(solution)/shard_map/while/body/eval_jaxpr/ppermute | solution.py:10
  170.6 5.8 %collective-permute-done.1 = f32[28,1152]{1,0:T(8,128)S(1)} collective-permute-done((f32[28,1152]{1,0:T(8,128)S(1)}, f32[28,1152]{1,0:T(8,128)S(1)}, u32[]{:S(2)}, u32[]{:S(2)}) %collective-permute-start.1) | collective-permute-done | bytes 129056 | tf_op jit(solution)/shard_map/while/body/eval_jaxpr/ppermute | solution.py:10
  178.4 2.7 bitcast_dynamic-update-slice_fusion.6
  185.5 6.6 %collective-permute-done.1 = f32[28,1152]{1,0:T(8,128)S(1)} collective-permute-done((f32[28,1152]{1,0:T(8,128)S(1)}, f32[28,1152]{1,0:T(8,128)S(1)}, u32[]{:S(2)}, u32[]{:S(2)}) %collective-permute-start.1) | collective-permute-done | bytes 129056 | tf_op jit(solution)/shard_map/while/body/eval_jaxpr/ppermute | solution.py:10
  194.0 2.7 bitcast_dynamic-update-slice_fusion.6
  201.1 6.7 %collective-permute-done.1 = f32[28,1152]{1,0:T(8,128)S(1)} collective-permute-done((f32[28,1152]{1,0:T(8,128)S(1)}, f32[28,1152]{1,0:T(8,128)S(1)}, u32[]{:S(2)}, u32[]{:S(2)}) %collective-permute-start.1) | collective-permute-done | bytes 129056 | tf_op jit(solution)/shard_map/while/body/eval_jaxpr/ppermute | solution.py:10
  216.8 6.8 %collective-permute-done.1 = f32[28,1152]{1,0:T(8,128)S(1)} collective-permute-done((f32[28,1152]{1,0:T(8,128)S(1)}, f32[28,1152]{1,0:T(8,128)S(1)}, u32[]{:S(2)}, u32[]{:S(2)}) %collective-permute-start.1) | collective-permute-done | bytes 129056 | tf_op jit(solution)/shard_map/while/body/eval_jaxpr/ppermute | solution.py:10
  232.6 6.6 %collective-permute-done.1 = f32[28,1152]{1,0:T(8,128)S(1)} collective-permute-done((f32[28,1152]{1,0:T(8,128)S(1)}, f32[28,1152]{1,0:T(8,128)S(1)}, u32[]{:S(2)}, u32[]{:S(2)}) %collective-permute-start.1) | collective-permute-done | bytes 129056 | tf_op jit(solution)/shard_map/while/body/eval_jaxpr/ppermute | solution.py:10
  248.2 6.1 %collective-permute-done.1 = f32[28,1152]{1,0:T(8,128)S(1)} collective-permute-done((f32[28,1152]{1,0:T(8,128)S(1)}, f32[28,1152]{1,0:T(8,128)S(1)}, u32[]{:S(2)}, u32[]{:S(2)}) %collective-permute-start.1) | collective-permute-done | bytes 129056 | tf_op jit(solution)/shard_map/while/body/eval_jaxpr/ppermute | solution.py:10
  263.3 5.8 %collective-permute-done.1 = f32[28,1152]{1,0:T(8,128)S(1)} collective-permute-done((f32[28,1152]{1,0:T(8,128)S(1)}, f32[28,1152]{1,0:T(8,128)S(1)}, u32[]{:S(2)}, u32[]{:S(2)}) %collective-permute-start.1) | collective-permute-done | bytes 129056 | tf_op jit(solution)/shard_map/while/body/eval_jaxpr/ppermute | solution.py:10
  278.2 5.8 %collective-permute-done.1 = f32[28,1152]{1,0:T(8,128)S(1)} collective-permute-done((f32[28,1152]{1,0:T(8,128)S(1)}, f32[28,1152]{1,0:T(8,128)S(1)}, u32[]{:S(2)}, u32[]{:S(2)}) %collective-permute-start.1) | collective-permute-done | bytes 129056 | tf_op jit(solution)/shard_map/while/body/eval_jaxpr/ppermute | solution.py:10
  286.0 2.7 bitcast_dynamic-update-slice_fusion.6
  293.4 5.5 %collective-permute-done.1 = f32[28,1152]{1,0:T(8,128)S(1)} collective-permute-done((f32[28,1152]{1,0:T(8,128)S(1)}, f32[28,1152]{1,0:T(8,128)S(1)}, u32[]{:S(2)}, u32[]{:S(2)}) %collective-permute-start.1) | collective-permute-done | bytes 129056 | tf_op jit(solution)/shard_map/while/body/eval_jaxpr/ppermute | solution.py:10
  300.8 2.7 bitcast_dynamic-update-slice_fusion.6
  308.8 5.0 collective-permute-done.1
  315.7 2.7 bitcast_dynamic-update-slice_fusion.6
  322.7 5.8 %collective-permute-done.1 = f32[28,1152]{1,0:T(8,128)S(1)} collective-permute-done((f32[28,1152]{1,0:T(8,128)S(1)}, f32[28,1152]{1,0:T(8,128)S(1)}, u32[]{:S(2)}, u32[]{:S(2)}) %collective-permute-start.1) | collective-permute-done | bytes 129056 | tf_op jit(solution)/shard_map/while/body/eval_jaxpr/ppermute | solution.py:10
  330.5 2.7 bitcast_dynamic-update-slice_fusion.6
  337.6 5.9 %collective-permute-done.1 = f32[28,1152]{1,0:T(8,128)S(1)} collective-permute-done((f32[28,1152]{1,0:T(8,128)S(1)}, f32[28,1152]{1,0:T(8,128)S(1)}, u32[]{:S(2)}, u32[]{:S(2)}) %collective-permute-start.1) | collective-permute-done | bytes 129056 | tf_op jit(solution)/shard_map/while/body/eval_jaxpr/ppermute | solution.py:10
  347.8 4.6 convolution_bitcast_fusion
  352.4 114.8 %fusion.2 = f32[32,1152]{1,0:T(8,128)S(1)} fusion(f32[896,1152]{1,0:T(8,128)} %convolution_bitcast_fusion), kind=kCustom, calls=%all-reduce-scatter | all-reduce-scatter fusion | flops 1179649 | bytes 4278272
  474.7 15.6 %all-to-all-start.1 = ((f32[32,2,1152]{2,1,0:T(2,128)}), f32[32,2,1152]{2,1,0:T(2,128)S(1)}, u32[]{:S(2)}, u32[]{:S(2)}) async-start(f32[32,2,1152]{2,1,0:T(2,128)} %reshape.136), calls=%async_computation.1 | async-start | bytes 589824 | tf_op jit(solution)/shard_map/all_to_all | solution.py:132
  492.0 11.9 %all-to-all-done.1 = f32[32,2,1152]{2,1,0:T(2,128)S(1)} async-done(((f32[32,2,1152]{2,1,0:T(2,128)}), f32[32,2,1152]{2,1,0:T(2,128)S(1)}, u32[]{:S(2)}, u32[]{:S(2)}) %all-to-all-start.1) | async-done | bytes 294944 | tf_op jit(solution)/shard_map/all_to_all | solution.py:132
  (167 shorter events, 143.5 us)
Async XLA Ops:
  7.2 103.2 %all-gather.3.cloned.1.call-start = ((), (), s32[]{:S(2)}) async-start(), calls=%async_computation.2 | async-start | bytes 2433024 | tf_op jit(solution)/shard_map/all_gather | solution.py:85
  13.2 44.4 %all-to-all-start = ((bf16[32,2,1152]{2,1,0:T(2,128)(2,1)}), bf16[32,2,1152]{2,1,0:T(2,128)(2,1)S(1)}, u32[]{:S(2)}, u32[]{:S(2)}) async-start(bf16[32,2,1152]{2,1,0:T(2,128)(2,1)} %reshape.134), calls=%async_computation | async-start | bytes 294912 | tf_op jit(solution)/shard_map/all_to_all | solution.py:74
  115.1 9.9 %collective-permute-start = (bf16[28,1152]{1,0:T(8,128)(2,1)S(1)}, bf16[28,1152]{1,0:T(8,128)(2,1)S(1)}, u32[]{:S(2)}, u32[]{:S(2)}) collective-permute-start(bf16[28,1152]{1,0:T(8,128)(2,1)S(1)} %copy.28), channel_id=1, source_target_pairs={{480,0},{0,32},{32,64},{64,96},{96,128},{128,160},{160,192},{192,2... | collective-permute-start | bytes 193544 | tf_op jit(solution)/shard_map/while/body/eval_jaxpr/ppermute | solution.py:10
  121.3 10.7 %collective-permute-start.1 = (f32[28,1152]{1,0:T(8,128)S(1)}, f32[28,1152]{1,0:T(8,128)S(1)}, u32[]{:S(2)}, u32[]{:S(2)}) collective-permute-start(f32[28,1152]{1,0:T(8,128)S(1)} %convolution_add_fusion.3), channel_id=1, source_target_pairs={{480,0},{0,32},{32,64},{64,96},{96,128},{128,160},{160,192},{192,2... | collective-permute-start | bytes 387080 | tf_op jit(solution)/shard_map/while/body/eval_jaxpr/ppermute | solution.py:10
  131.9 9.0 %collective-permute-start = (bf16[28,1152]{1,0:T(8,128)(2,1)S(1)}, bf16[28,1152]{1,0:T(8,128)(2,1)S(1)}, u32[]{:S(2)}, u32[]{:S(2)}) collective-permute-start(bf16[28,1152]{1,0:T(8,128)(2,1)S(1)} %copy.28), channel_id=1, source_target_pairs={{480,0},{0,32},{32,64},{64,96},{96,128},{128,160},{160,192},{192,2... | collective-permute-start | bytes 193544 | tf_op jit(solution)/shard_map/while/body/eval_jaxpr/ppermute | solution.py:10
  137.0 9.8 %collective-permute-start.1 = (f32[28,1152]{1,0:T(8,128)S(1)}, f32[28,1152]{1,0:T(8,128)S(1)}, u32[]{:S(2)}, u32[]{:S(2)}) collective-permute-start(f32[28,1152]{1,0:T(8,128)S(1)} %convolution_add_fusion.3), channel_id=1, source_target_pairs={{480,0},{0,32},{32,64},{64,96},{96,128},{128,160},{160,192},{192,2... | collective-permute-start | bytes 387080 | tf_op jit(solution)/shard_map/while/body/eval_jaxpr/ppermute | solution.py:10
  146.8 9.0 %collective-permute-start = (bf16[28,1152]{1,0:T(8,128)(2,1)S(1)}, bf16[28,1152]{1,0:T(8,128)(2,1)S(1)}, u32[]{:S(2)}, u32[]{:S(2)}) collective-permute-start(bf16[28,1152]{1,0:T(8,128)(2,1)S(1)} %copy.28), channel_id=1, source_target_pairs={{480,0},{0,32},{32,64},{64,96},{96,128},{128,160},{160,192},{192,2... | collective-permute-start | bytes 193544 | tf_op jit(solution)/shard_map/while/body/eval_jaxpr/ppermute | solution.py:10
  151.8 9.8 %collective-permute-start.1 = (f32[28,1152]{1,0:T(8,128)S(1)}, f32[28,1152]{1,0:T(8,128)S(1)}, u32[]{:S(2)}, u32[]{:S(2)}) collective-permute-start(f32[28,1152]{1,0:T(8,128)S(1)} %convolution_add_fusion.3), channel_id=1, source_target_pairs={{480,0},{0,32},{32,64},{64,96},{96,128},{128,160},{160,192},{192,2... | collective-permute-start | bytes 387080 | tf_op jit(solution)/shard_map/while/body/eval_jaxpr/ppermute | solution.py:10
  166.7 9.8 %collective-permute-start.1 = (f32[28,1152]{1,0:T(8,128)S(1)}, f32[28,1152]{1,0:T(8,128)S(1)}, u32[]{:S(2)}, u32[]{:S(2)}) collective-permute-start(f32[28,1152]{1,0:T(8,128)S(1)} %convolution_add_fusion.3), channel_id=1, source_target_pairs={{480,0},{0,32},{32,64},{64,96},{96,128},{128,160},{160,192},{192,2... | collective-permute-start | bytes 387080 | tf_op jit(solution)/shard_map/while/body/eval_jaxpr/ppermute | solution.py:10
  176.5 9.0 %collective-permute-start = (bf16[28,1152]{1,0:T(8,128)(2,1)S(1)}, bf16[28,1152]{1,0:T(8,128)(2,1)S(1)}, u32[]{:S(2)}, u32[]{:S(2)}) collective-permute-start(bf16[28,1152]{1,0:T(8,128)(2,1)S(1)} %copy.28), channel_id=1, source_target_pairs={{480,0},{0,32},{32,64},{64,96},{96,128},{128,160},{160,192},{192,2... | collective-permute-start | bytes 193544 | tf_op jit(solution)/shard_map/while/body/eval_jaxpr/ppermute | solution.py:10
  181.5 10.6 %collective-permute-start.1 = (f32[28,1152]{1,0:T(8,128)S(1)}, f32[28,1152]{1,0:T(8,128)S(1)}, u32[]{:S(2)}, u32[]{:S(2)}) collective-permute-start(f32[28,1152]{1,0:T(8,128)S(1)} %convolution_add_fusion.3), channel_id=1, source_target_pairs={{480,0},{0,32},{32,64},{64,96},{96,128},{128,160},{160,192},{192,2... | collective-permute-start | bytes 387080 | tf_op jit(solution)/shard_map/while/body/eval_jaxpr/ppermute | solution.py:10
  192.1 9.0 %collective-permute-start = (bf16[28,1152]{1,0:T(8,128)(2,1)S(1)}, bf16[28,1152]{1,0:T(8,128)(2,1)S(1)}, u32[]{:S(2)}, u32[]{:S(2)}) collective-permute-start(bf16[28,1152]{1,0:T(8,128)(2,1)S(1)} %copy.28), channel_id=1, source_target_pairs={{480,0},{0,32},{32,64},{64,96},{96,128},{128,160},{160,192},{192,2... | collective-permute-start | bytes 193544 | tf_op jit(solution)/shard_map/while/body/eval_jaxpr/ppermute | solution.py:10
  197.1 10.7 %collective-permute-start.1 = (f32[28,1152]{1,0:T(8,128)S(1)}, f32[28,1152]{1,0:T(8,128)S(1)}, u32[]{:S(2)}, u32[]{:S(2)}) collective-permute-start(f32[28,1152]{1,0:T(8,128)S(1)} %convolution_add_fusion.3), channel_id=1, source_target_pairs={{480,0},{0,32},{32,64},{64,96},{96,128},{128,160},{160,192},{192,2... | collective-permute-start | bytes 387080 | tf_op jit(solution)/shard_map/while/body/eval_jaxpr/ppermute | solution.py:10
  207.8 9.0 %collective-permute-start = (bf16[28,1152]{1,0:T(8,128)(2,1)S(1)}, bf16[28,1152]{1,0:T(8,128)(2,1)S(1)}, u32[]{:S(2)}, u32[]{:S(2)}) collective-permute-start(bf16[28,1152]{1,0:T(8,128)(2,1)S(1)} %copy.28), channel_id=1, source_target_pairs={{480,0},{0,32},{32,64},{64,96},{96,128},{128,160},{160,192},{192,2... | collective-permute-start | bytes 193544 | tf_op jit(solution)/shard_map/while/body/eval_jaxpr/ppermute | solution.py:10
  212.8 10.8 %collective-permute-start.1 = (f32[28,1152]{1,0:T(8,128)S(1)}, f32[28,1152]{1,0:T(8,128)S(1)}, u32[]{:S(2)}, u32[]{:S(2)}) collective-permute-start(f32[28,1152]{1,0:T(8,128)S(1)} %convolution_add_fusion.3), channel_id=1, source_target_pairs={{480,0},{0,32},{32,64},{64,96},{96,128},{128,160},{160,192},{192,2... | collective-permute-start | bytes 387080 | tf_op jit(solution)/shard_map/while/body/eval_jaxpr/ppermute | solution.py:10
  223.6 9.0 %collective-permute-start = (bf16[28,1152]{1,0:T(8,128)(2,1)S(1)}, bf16[28,1152]{1,0:T(8,128)(2,1)S(1)}, u32[]{:S(2)}, u32[]{:S(2)}) collective-permute-start(bf16[28,1152]{1,0:T(8,128)(2,1)S(1)} %copy.28), channel_id=1, source_target_pairs={{480,0},{0,32},{32,64},{64,96},{96,128},{128,160},{160,192},{192,2... | collective-permute-start | bytes 193544 | tf_op jit(solution)/shard_map/while/body/eval_jaxpr/ppermute | solution.py:10
  228.6 10.6 %collective-permute-start.1 = (f32[28,1152]{1,0:T(8,128)S(1)}, f32[28,1152]{1,0:T(8,128)S(1)}, u32[]{:S(2)}, u32[]{:S(2)}) collective-permute-start(f32[28,1152]{1,0:T(8,128)S(1)} %convolution_add_fusion.3), channel_id=1, source_target_pairs={{480,0},{0,32},{32,64},{64,96},{96,128},{128,160},{160,192},{192,2... | collective-permute-start | bytes 387080 | tf_op jit(solution)/shard_map/while/body/eval_jaxpr/ppermute | solution.py:10
  244.2 10.1 %collective-permute-start.1 = (f32[28,1152]{1,0:T(8,128)S(1)}, f32[28,1152]{1,0:T(8,128)S(1)}, u32[]{:S(2)}, u32[]{:S(2)}) collective-permute-start(f32[28,1152]{1,0:T(8,128)S(1)} %convolution_add_fusion.3), channel_id=1, source_target_pairs={{480,0},{0,32},{32,64},{64,96},{96,128},{128,160},{160,192},{192,2... | collective-permute-start | bytes 387080 | tf_op jit(solution)/shard_map/while/body/eval_jaxpr/ppermute | solution.py:10
  259.4 9.8 %collective-permute-start.1 = (f32[28,1152]{1,0:T(8,128)S(1)}, f32[28,1152]{1,0:T(8,128)S(1)}, u32[]{:S(2)}, u32[]{:S(2)}) collective-permute-start(f32[28,1152]{1,0:T(8,128)S(1)} %convolution_add_fusion.3), channel_id=1, source_target_pairs={{480,0},{0,32},{32,64},{64,96},{96,128},{128,160},{160,192},{192,2... | collective-permute-start | bytes 387080 | tf_op jit(solution)/shard_map/while/body/eval_jaxpr/ppermute | solution.py:10
  274.2 9.8 %collective-permute-start.1 = (f32[28,1152]{1,0:T(8,128)S(1)}, f32[28,1152]{1,0:T(8,128)S(1)}, u32[]{:S(2)}, u32[]{:S(2)}) collective-permute-start(f32[28,1152]{1,0:T(8,128)S(1)} %convolution_add_fusion.3), channel_id=1, source_target_pairs={{480,0},{0,32},{32,64},{64,96},{96,128},{128,160},{160,192},{192,2... | collective-permute-start | bytes 387080 | tf_op jit(solution)/shard_map/while/body/eval_jaxpr/ppermute | solution.py:10
  284.0 9.3 %collective-permute-start = (bf16[28,1152]{1,0:T(8,128)(2,1)S(1)}, bf16[28,1152]{1,0:T(8,128)(2,1)S(1)}, u32[]{:S(2)}, u32[]{:S(2)}) collective-permute-start(bf16[28,1152]{1,0:T(8,128)(2,1)S(1)} %copy.28), channel_id=1, source_target_pairs={{480,0},{0,32},{32,64},{64,96},{96,128},{128,160},{160,192},{192,2... | collective-permute-start | bytes 193544 | tf_op jit(solution)/shard_map/while/body/eval_jaxpr/ppermute | solution.py:10
  289.1 9.8 %collective-permute-start.1 = (f32[28,1152]{1,0:T(8,128)S(1)}, f32[28,1152]{1,0:T(8,128)S(1)}, u32[]{:S(2)}, u32[]{:S(2)}) collective-permute-start(f32[28,1152]{1,0:T(8,128)S(1)} %convolution_add_fusion.3), channel_id=1, source_target_pairs={{480,0},{0,32},{32,64},{64,96},{96,128},{128,160},{160,192},{192,2... | collective-permute-start | bytes 387080 | tf_op jit(solution)/shard_map/while/body/eval_jaxpr/ppermute | solution.py:10
  298.9 9.9 %collective-permute-start = (bf16[28,1152]{1,0:T(8,128)(2,1)S(1)}, bf16[28,1152]{1,0:T(8,128)(2,1)S(1)}, u32[]{:S(2)}, u32[]{:S(2)}) collective-permute-start(bf16[28,1152]{1,0:T(8,128)(2,1)S(1)} %copy.28), channel_id=1, source_target_pairs={{480,0},{0,32},{32,64},{64,96},{96,128},{128,160},{160,192},{192,2... | collective-permute-start | bytes 193544 | tf_op jit(solution)/shard_map/while/body/eval_jaxpr/ppermute | solution.py:10
  303.9 9.8 %collective-permute-start.1 = (f32[28,1152]{1,0:T(8,128)S(1)}, f32[28,1152]{1,0:T(8,128)S(1)}, u32[]{:S(2)}, u32[]{:S(2)}) collective-permute-start(f32[28,1152]{1,0:T(8,128)S(1)} %convolution_add_fusion.3), channel_id=1, source_target_pairs={{480,0},{0,32},{32,64},{64,96},{96,128},{128,160},{160,192},{192,2... | collective-permute-start | bytes 387080 | tf_op jit(solution)/shard_map/while/body/eval_jaxpr/ppermute | solution.py:10
  318.8 9.8 %collective-permute-start.1 = (f32[28,1152]{1,0:T(8,128)S(1)}, f32[28,1152]{1,0:T(8,128)S(1)}, u32[]{:S(2)}, u32[]{:S(2)}) collective-permute-start(f32[28,1152]{1,0:T(8,128)S(1)} %convolution_add_fusion.3), channel_id=1, source_target_pairs={{480,0},{0,32},{32,64},{64,96},{96,128},{128,160},{160,192},{192,2... | collective-permute-start | bytes 387080 | tf_op jit(solution)/shard_map/while/body/eval_jaxpr/ppermute | solution.py:10
  333.6 9.8 %collective-permute-start.1 = (f32[28,1152]{1,0:T(8,128)S(1)}, f32[28,1152]{1,0:T(8,128)S(1)}, u32[]{:S(2)}, u32[]{:S(2)}) collective-permute-start(f32[28,1152]{1,0:T(8,128)S(1)} %convolution_add_fusion.3), channel_id=1, source_target_pairs={{480,0},{0,32},{32,64},{64,96},{96,128},{128,160},{160,192},{192,2... | collective-permute-start | bytes 387080 | tf_op jit(solution)/shard_map/while/body/eval_jaxpr/ppermute | solution.py:10
  345.9 127.3 %collective-permute-start.2 = (f32[28,1152]{1,0:T(8,128)S(1)}, f32[28,1152]{1,0:T(8,128)S(1)}, u32[]{:S(2)}, u32[]{:S(2)}) collective-permute-start(f32[28,1152]{1,0:T(8,128)S(1)} %convolution_add_fusion.1), channel_id=1, source_target_pairs={{480,0},{0,32},{32,64},{64,96},{96,128},{128,160},{160,192},{192,2... | collective-permute-start | bytes 387080 | tf_op jit(solution)/shard_map/ppermute | solution.py:10
  467.3 23.0 %collective-permute-start.5 = (f32[32,1152]{1,0:T(8,128)S(1)}, f32[32,1152]{1,0:T(8,128)S(1)}, u32[]{:S(2)}, u32[]{:S(2)}) collective-permute-start(f32[32,1152]{1,0:T(8,128)S(1)} %fusion.2), channel_id=1, source_target_pairs={{0,3},{1,4},{2,5},{3,6},{4,7},{5,8},{6,9},{7,10},{8,11},{9,12},{10... | collective-permute-start | bytes 442376
  468.6 21.7 %collective-permute-start.4 = (f32[32,1152]{1,0:T(8,128)S(1)}, f32[32,1152]{1,0:T(8,128)S(1)}, u32[]{:S(2)}, u32[]{:S(2)}) collective-permute-start(f32[32,1152]{1,0:T(8,128)S(1)} %fusion.2), channel_id=1, source_target_pairs={{0,2},{1,3},{2,4},{3,5},{4,6},{5,7},{6,8},{7,9},{8,10},{9,11},{10,... | collective-permute-start | bytes 442376
  469.9 20.4 %collective-permute-start.3 = (f32[32,1152]{1,0:T(8,128)S(1)}, f32[32,1152]{1,0:T(8,128)S(1)}, u32[]{:S(2)}, u32[]{:S(2)}) collective-permute-start(f32[32,1152]{1,0:T(8,128)S(1)} %fusion.2), channel_id=1, source_target_pairs={{0,1},{1,2},{2,3},{3,4},{4,5},{5,6},{6,7},{7,8},{8,9},{9,10},{10,1... | collective-permute-start | bytes 442376
  471.8 18.4 %collective-permute-start.6 = (f32[28,1152]{1,0:T(8,128)S(1)}, f32[28,1152]{1,0:T(8,128)S(1)}, u32[]{:S(2)}, u32[]{:S(2)}) collective-permute-start(f32[28,1152]{1,0:T(8,128)S(1)} %slice), channel_id=1, source_target_pairs={{0,4},{1,5},{2,6},{3,7},{4,8},{5,9},{6,10},{7,11},{8,12},{9,13},{1... | collective-permute-start | bytes 387080
  474.7 29.2 %all-to-all-start.1 = ((f32[32,2,1152]{2,1,0:T(2,128)}), f32[32,2,1152]{2,1,0:T(2,128)S(1)}, u32[]{:S(2)}, u32[]{:S(2)}) async-start(f32[32,2,1152]{2,1,0:T(2,128)} %reshape.136), calls=%async_computation.1 | async-start | bytes 589824 | tf_op jit(solution)/shard_map/all_to_all | solution.py:132
  (9 other events, 85.3 us)
Sparse Core Ops, SparseCore 0:
  11.9 98.4 all-gather.2
where the time goes:
time: 514 us; the launch traced here: 512 us
  waiting for transfers between devices  175 us (34%)
  blocking collectives  133 us (26%)
  starting transfers between devices  101 us (20%)
  matrix products  55.6 us (11%)
  local copies, waits for them, and re-layouts  21.1 us (4%)
  between operations  17.5 us (3%)
  other arithmetic  8.06 us (2%)
    unnamed x2, blocking collectives  133 us
    ppermute x31, waiting for transfers between devices, passed_along(): return lax.ppermute(block, axis, route)  111 us
    ppermute x31, starting transfers between devices, passed_along(): return lax.ppermute(block, axis, route)  62.3 us
    all_gather x1, waiting for transfers between devices, shards(): lax.all_gather(text_unit.astype(jnp.bfloat16), 'grp', axis=0, tiled=True)  52.4 us
    dot_general x16, matrix products, stop_terms(): lax.dot_general(images_here, group_text, (((1,), (1,)), ((), ())), prefer...  41.1 us
    all_to_all x1, starting transfers between devices, shards(): lax.all_to_all(sending.reshape(groups, per_owner, width), 'grp', split_ax...  17.2 us
    all_to_all x1, starting transfers between devices, shards(): lax.all_to_all(outgoing.reshape(groups, per_owner, width), 'grp', split_a...  15.6 us
    all_to_all x1, waiting for transfers between devices, shards(): lax.all_to_all(outgoing.reshape(groups, per_owner, width), 'grp', split_a...  11.9 us
  transfers between devices with their start and end apart: 38, of which 31 were waited for; matrix products, arithmetic and copies ran while one was open for 37% of the time, Pallas kernels for 0%

commit v1 on v0

v1 whole, which is shorter than its diff:
```python
import jax
import jax.numpy as jnp
from jax import lax
from jax.experimental import pallas as pl
from jax.experimental.pallas import tpu as pltpu
from jax.sharding import PartitionSpec as P

MESH = pl.DeviceIdType.MESH
F32 = jnp.float32
BF16 = jnp.bfloat16
ORDER = (0, 1, -1, 2, -2, 3, -3, 4)
MESSAGES = 160


def pos(offset):
    return ORDER.index(4 if offset == -4 else offset)


def unit_rows(values):
    wide = values.astype(F32)
    inverse = lax.rsqrt(jnp.sum(wide * wide, axis=-1, keepdims=True) + 1e-06)
    return wide * inverse, inverse


def unit_back(grad, unit, inverse):
    return (grad - unit * jnp.sum(unit * grad, axis=-1, keepdims=True)) * inverse


def kernel(
    img_ref, own_ref, cnt_ref, text_ref, scale_ref, bias_ref,
    ig_ref, tg_ref,
    img, ids, id_own, id_sib, txt, dst, tu,
    gown, gsend, grecv, zs, zr_, ta, as_, ar_, axs, axr, tb, bxs, bxr, bys, byr,
    ssem, rsem,
):
    width = img_ref.shape[1]
    cap = img_ref.shape[0]
    pairs = text_ref.shape[0]
    blk = lax.axis_index("blk")
    grp = lax.axis_index("grp")
    x, y = blk % 4, (grp // 16) * 4 + blk // 4
    z, c = (grp // 2) % 8, grp % 2

    def device(x, y, z, c):
        return ((y % 4) * 4 + x, (y // 4) * 16 + z * 2 + c)

    zp, zm = device(x, y, (z + 1) % 8, c), device(x, y, (z + 7) % 8, c)
    yp, ym = device(x, (y + 1) % 8, z, c), device(x, (y + 7) % 8, z, c)
    core = device(x, y, z, 1 - c)
    xk = {k: device((x + k) % 4, y, z, c) for k in (1, 2, 3)}

    barrier = pltpu.get_barrier_semaphore()
    partners = [zp, zm, yp, ym, core, xk[1], xk[2], xk[3]]
    for p in partners:
        pl.semaphore_signal(barrier, inc=1, device_id=p, device_id_type=MESH)

    sent = []

    def send(src, dst_, where):
        i = len(sent)
        copy = pltpu.make_async_remote_copy(
            src_ref=src, dst_ref=dst_, send_sem=ssem.at[i], recv_sem=rsem.at[i],
            device_id=where, device_id_type=MESH,
        )
        copy.start()
        sent.append(copy)
        return copy

    def arrive(copies):
        for copy in copies:
            copy.wait_recv()

    live = lax.broadcasted_iota(jnp.int32, (cap, 1), 0) < cnt_ref[0]
    image_unit, image_inv = unit_rows(img_ref[...])
    img[0, 0] = jnp.where(live, image_unit, 0.0).astype(BF16)
    lane = lax.broadcasted_iota(jnp.int32, (8, 128), 1)
    slot = jnp.where(lane < cap, lane, lane - cap)
    id_own[...] = jnp.where(slot < cnt_ref[0], jnp.broadcast_to(own_ref[...], (8, 128)), -2)
    text_unit, text_inv = unit_rows(text_ref[...])
    tu[...] = jnp.zeros_like(tu)
    tu[0:pairs] = text_unit
    txt[0, 0, 0] = tu[0:16].astype(BF16)
    txt[1, 0, 0] = tu[16:32].astype(BF16)

    pl.semaphore_wait(barrier, len(partners))

    def z_hop(h):
        if h < 4:
            return [
                send(img.at[pos(1 - h), 0], img.at[pos(-h), 0], zp),
                send(img.at[pos(h - 1), 0], img.at[pos(h), 0], zm),
            ]
        return [
            send(img.at[pos(-3), 0, pl.ds(0, 32)], img.at[7, 0, pl.ds(0, 32)], zp),
            send(img.at[pos(3), 0, pl.ds(32, 32)], img.at[7, 0, pl.ds(32, 32)], zm),
        ]

    def id_hop(h):
        out = [send(ids.at[pos(1 - h)], ids.at[pos(-h)], zp)]
        if h < 4:
            out.append(send(ids.at[pos(h - 1)], ids.at[pos(h)], zm))
        return out

    def core_pass(first, n):
        return [send(img.at[pl.ds(first, n), 0], img.at[pl.ds(first, n), 1], core)]

    def a_across():
        return [send(txt.at[0, 0, 0], txt.at[0, 0, 4 - k], xk[k]) for k in (1, 2, 3)]

    def a_hop(h):
        if h < 4:
            return [
                send(txt.at[0, pos(1 - h)], txt.at[0, pos(-h)], yp),
                send(txt.at[0, pos(h - 1)], txt.at[0, pos(h)], ym),
            ]
        return [
            send(txt.at[0, pos(-3), pl.ds(0, 2)], txt.at[0, 7, pl.ds(0, 2)], yp),
            send(txt.at[0, pos(3), pl.ds(2, 2)], txt.at[0, 7, pl.ds(2, 2)], ym),
        ]

    def b_hop(h):
        out = [send(txt.at[1, pos(1 - h), 0], txt.at[1, pos(-h), 0], yp)]
        if h < 4:
            out.append(send(txt.at[1, pos(h - 1), 0], txt.at[1, pos(h), 0], ym))
        return out

    def b_across(first, n):
        return [
            send(txt.at[1, pl.ds(first, n), 0], txt.at[1, pl.ds(first, n), 4 - k], xk[k])
            for k in (1, 2, 3)
        ]

    scale = scale_ref[0]
    bias = bias_ref[0]

    def score(half, gt, gi):
        texts = txt[half, 2 * gt : 2 * gt + 2].reshape(128, width)
        images = img[2 * gi : 2 * gi + 2].reshape(4 * cap, width)
        raw = lax.dot_general(
            texts, images, (((1,), (1,)), ((), ())), preferred_element_type=F32
        )
        e = jnp.exp(-(scale * raw + bias))
        slope = 1.0 / (1.0 + e)
        if gt in (0, 3):
            at = 0 if gt == 0 else 64
            half_y = y // 4 if gt == 0 else 1 - y // 4
            owner = half_y * 16 + z * 2 + c
            row = lax.broadcasted_iota(jnp.int32, (128, 1), 0) - at
            named = (row >= 0) & (row < 16) & (row + 16 * half < pairs)
            row_id = jnp.where(named, owner * pairs + 16 * half + row, -1)
            column_id = jnp.concatenate([ids[2 * gi, 0:1], ids[2 * gi + 1, 0:1]], axis=1)
            slope = jnp.where(row_id == column_id, -e * slope, slope)
        dst[
            half * 512 + gt * 128 : half * 512 + gt * 128 + 128, gi * 256 : gi * 256 + 256
        ] = (scale * slope).astype(BF16)

    def scores(s):
        for gi in range(s + 1):
            for half in (0, 1):
                score(half, s, gi)
        for gt in range(s):
            for half in (0, 1):
                score(half, gt, s)

    zw = z_hop(1)
    idw = [send(id_own, id_sib, core)]
    aw = a_across()
    bw = b_hop(1)
    spans = ((0, 1), (1, 2), (3, 2), (5, 2), (7, 1))
    cw, bx = [core_pass(0, 1)], [b_across(0, 1)]
    arrive(idw)
    ids[0] = jnp.where(lane < cap, id_own[...], id_sib[...])
    idw = id_hop(1)
    arrive(aw)
    aw = a_hop(1)
    arrive(cw[0] + bx[0])
    for h in (1, 2, 3, 4):
        arrive(zw)
        if h < 4:
            zw = z_hop(h + 1)
        cw.append(core_pass(*spans[h]))
        arrive(bw)
        if h < 4:
            bw = b_hop(h + 1)
        bx.append(b_across(*spans[h]))
        arrive(idw)
        if h < 4:
            idw = id_hop(h + 1)
        arrive(aw)
        if h < 4:
            aw = a_hop(h + 1)
        if h > 1:
            arrive(cw[h - 1] + bx[h - 1])
            scores(h - 2)
    arrive(cw[4] + bx[4])
    scores(3)

    def image_part(gi):
        g = lax.dot_general(
            dst[:, gi * 256 : gi * 256 + 256], txt[...].reshape(1024, width),
            (((0,), (0,)), ((), ())), preferred_element_type=F32,
        ).reshape(2, 2, cap, width)
        gown[2 * gi : 2 * gi + 2] = g[:, 0]
        gsend[2 * gi : 2 * gi + 2] = g[:, 1].astype(BF16)
        return [send(gsend.at[pl.ds(2 * gi, 2)], grecv.at[pl.ds(2 * gi, 2)], core)]

    def text_part(half, gt):
        images = img[...].reshape(16 * cap, width)
        t = jnp.dot(
            dst[half * 512 + gt * 128 : half * 512 + gt * 128 + 128, :], images,
            preferred_element_type=F32,
        )
        if half == 0:
            ta[2 * gt : 2 * gt + 2] = t.reshape(2, 64, width)
            return []
        t = t.reshape(2, 4, 16, width)
        tb[2 * gt : 2 * gt + 2] = t[:, 0]
        bxs[2 * gt : 2 * gt + 2] = t[:, 1:].astype(BF16)
        two = pl.ds(2 * gt, 2)
        return [send(bxs.at[two, k - 1], bxr.at[two, k - 1], xk[k]) for k in (1, 2, 3)]

    def image_sum(p, j):
        rows = pl.ds(32 * j, 32)
        return gown[p, rows] + grecv[p, rows].astype(F32)

    def a_sum(p, j):
        return ta[p, pl.ds(32 * j, 32)]

    def hop_back(own, outs, ins, h, up, down):
        copies = []
        for side, sign, where in ((0, 1, up), (1, -1, down)):
            p = pos(sign * (5 - h))
            for j in (0, 1) if h > 1 else (side,):
                value = own(p, j)
                if h > 2 or (h == 2 and j == side):
                    value = value + ins[side, h - 2, j].astype(F32)
                outs[side, h - 1, j] = value.astype(BF16)
            if h > 1:
                copies.append(send(outs.at[side, h - 1], ins.at[side, h - 1], where))
            else:
                copies.append(send(outs.at[side, 0, side], ins.at[side, 0, side], where))
        return copies

    def b_sum(p):
        return tb[p] + bxr[p, 0].astype(F32) + bxr[p, 1].astype(F32) + bxr[p, 2].astype(F32)

    def b_back(h):
        copies = []
        for side, sign, where in ((0, 1, yp), (1, -1, ym)):
            if side == 1 and h == 1:
                continue
            value = b_sum(pos(sign * (5 - h)))
            if h > 1 + side:
                value = value + byr[side, h - 2].astype(F32)
            bys[side, h - 1] = value.astype(BF16)
            copies.append(send(bys.at[side, h - 1], byr.at[side, h - 1], where))
        return copies

    cores, across = {}, {}
    zw = aw = bw = []
    for h in (1, 2, 3, 4):
        g = 4 - h
        cores[g] = image_part(g)
        text_part(0, g)
        arrive(aw)
        aw = hop_back(a_sum, as_, ar_, h, yp, ym)
        across[g] = text_part(1, g)
        arrive(cores[g] + zw)
        zw = hop_back(image_sum, zs, zr_, h, zp, zm)
        arrive(across[g] + bw)
        bw = b_back(h)
    arrive(aw)
    own_a = [a_sum(0, j) + ar_[0, 3, j].astype(F32) + ar_[1, 3, j].astype(F32) for j in (0, 1)]
    for k in (1, 2, 3):
        axs[k - 1] = own_a[k // 2][16 * (k % 2) : 16 * (k % 2) + 16].astype(BF16)
    ax = [send(axs.at[k - 1], axr.at[k - 1], xk[k]) for k in (1, 2, 3)]
    arrive(zw)
    total = jnp.concatenate(
        [image_sum(0, j) + zr_[0, 3, j].astype(F32) + zr_[1, 3, j].astype(F32) for j in (0, 1)]
    )
    ig_ref[...] = jnp.where(live, unit_back(total, image_unit, image_inv), 0.0)
    arrive(bw)
    total_b = b_sum(0) + byr[0, 3].astype(F32) + byr[1, 3].astype(F32)
    arrive(ax)
    total_a = own_a[0][0:16]
    for k in range(3):
        total_a = total_a + axr[k].astype(F32)
    total = jnp.concatenate([total_a, total_b])[0:pairs]
    tg_ref[...] = unit_back(total, tu[0:pairs], text_inv)
    for copy in sent:
        copy.wait_send()


def shards(tower_images, owners, counts, text, logit_scale, logit_bias):
    cap, width = tower_images.shape
    pairs = text.shape[0]
    twice = jnp.concatenate([owners, owners]).reshape(1, 2 * cap)
    vmem = pl.BlockSpec(memory_space=pltpu.VMEM)
    smem = pl.BlockSpec(memory_space=pltpu.SMEM)
    V = pltpu.VMEM
    return pl.pallas_call(
        kernel,
        out_shape=(
            jax.ShapeDtypeStruct((cap, width), F32),
            jax.ShapeDtypeStruct((pairs, width), F32),
        ),
        in_specs=[vmem, vmem, smem, vmem, smem, smem],
        out_specs=(vmem, vmem),
        scratch_shapes=[
            V((8, 2, cap, width), BF16),
            V((8, 8, 128), jnp.int32),
            V((8, 128), jnp.int32),
            V((8, 128), jnp.int32),
            V((2, 8, 4, 16, width), BF16),
            V((1024, 1024), BF16),
            V((32, width), F32),
            V((8, cap, width), F32),
            V((8, cap, width), BF16),
            V((8, cap, width), BF16),
            V((2, 4, 2, 32, width), BF16),
            V((2, 4, 2, 32, width), BF16),
            V((8, 64, width), F32),
            V((2, 4, 2, 32, width), BF16),
            V((2, 4, 2, 32, width), BF16),
            V((3, 16, width), BF16),
            V((3, 16, width), BF16),
            V((8, 16, width), F32),
            V((8, 3, 16, width), BF16),
            V((8, 3, 16, width), BF16),
            V((2, 4, 16, width), BF16),
            V((2, 4, 16, width), BF16),
            pltpu.SemaphoreType.DMA((MESSAGES,)),
            pltpu.SemaphoreType.DMA((MESSAGES,)),
        ],
        compiler_params=pltpu.CompilerParams(
            collective_id=0, has_side_effects=True, vmem_limit_bytes=56 << 20
        ),
    )(tower_images, twice, counts, text, logit_scale, logit_bias)


def solution(mesh):
    split = P(("blk", "grp"))
    rows = P(("blk", "grp"), None)
    return jax.shard_map(
        shards, mesh=mesh, in_specs=(rows, split, split, rows, P(), P()), out_specs=(rows, rows),
        check_vma=False,
    )
```

time: 514 us -> 85.3 us (0.17)
  the two profiles are of different devices: /device:TPU:1 before, /device:TPU:24 now
where the time goes in v1:
time: 85.3 us; the launch traced here: 85.1 us
  Pallas kernels  79.5 us (93%)
  between operations  2.62 us (3%)
  local copies, waits for them, and re-layouts  2.4 us (3%)
    pallas_call x1, Pallas kernels, shards(): pl.pallas_call(kernel, out_shape=(jax.ShapeDtypeStruct((cap, width), F32)...  79.5 us
    unnamed x6, local copies, waits for them, and re-layouts  2.4 us

profile of v1, /device:TPU:24, one launch (start us, length us, event | category | flops | bytes accessed | tf_op | source)
XLA Modules:
  0.0 85.1 jit_solution(5826906044779207894)
XLA Ops:
  1.9 0.0 copy-start.1
  2.6 0.0 copy-done.1
  2.6 0.6 add_bitcast_fusion.own_ref
  3.2 79.5 %shard_map.77 = (f32[64,1152]{1,0:T(8,128)}, f32[28,1152]{1,0:T(8,128)}) custom-call(bf16[64,1152]{1,0:T(8,128)(2,1)} %img_ref.1, s32[1,128]{1,0:T(1,128)} %add_bitcast_fusion.own_ref, s32[1]{0:T(128)S(6)} %copy.10.cnt_ref, bf16[28,1152]{1,0:T(8,128)(2,1)} %text_ref.1, f32[1]{0:T(128)S(6)} %copy.11.scale_ref, f32[1]{0:T(128)S(6)} %copy.12.bias_ref), custom_call_target="tpu_custom_call" | custom-call | tf_op jit(solution)/shard_map/pallas_call | solution.py:301
  82.7 0.0 copy-start
  82.7 1.7 %copy.13 = f32[64,1152]{1,0:T(8,128)} copy(f32[64,1152]{1,0:T(8,128)} %get-tuple-element.4) | data formatting | bytes 589824
  84.4 0.0 copy-done
  84.4 0.7 copy.14
Async XLA Ops:
  1.9 0.7 copy-start.1
  82.7 1.7 %copy-start = (f32[28,1152]{1,0:T(8,128)S(1)}, f32[28,1152]{1,0:T(8,128)}, u32[]{:S(2)}) copy-start(f32[28,1152]{1,0:T(8,128)} %get-tuple-element.5) | copy-start | bytes 387076

commit v2 on v1

v2 whole, which is shorter than its diff:
```python
import jax
import jax.numpy as jnp
from jax import lax
from jax.experimental import pallas as pl
from jax.experimental.pallas import tpu as pltpu
from jax.sharding import PartitionSpec as P

MESH = pl.DeviceIdType.MESH
F32 = jnp.float32
BF16 = jnp.bfloat16
ORDER = (0, 1, -1, 2, -2, 3, -3, 4)
UNITS = 32
SEMAPHORES = 100


def pos(offset):
    return ORDER.index(4 if offset == -4 else offset)


def unit_rows(values):
    wide = values.astype(F32)
    inverse = lax.rsqrt(jnp.sum(wide * wide, axis=-1, keepdims=True) + 1e-06)
    return wide * inverse, inverse


def unit_back(grad, unit, inverse):
    return (grad - unit * jnp.sum(unit * grad, axis=-1, keepdims=True)) * inverse


def kernel(
    img_ref, own_ref, cnt_ref, text_ref, scale_ref, bias_ref,
    ig_ref, tg_ref,
    img, ids, id_own, id_sib, txt, dst, tu,
    gown, gsend, grecv, zs, zr_, ta, as_, ar_, axs, axr, tb, bxs, bxr, bys, byr,
    sems,
):
    width = img_ref.shape[1]
    cap = img_ref.shape[0]
    pairs = text_ref.shape[0]
    blk = lax.axis_index("blk")
    grp = lax.axis_index("grp")
    x, y = blk % 4, (grp // 16) * 4 + blk // 4
    z, c = (grp // 2) % 8, grp % 2

    def device(x, y, z, c):
        return ((y % 4) * 4 + x, (y // 4) * 16 + z * 2 + c)

    zp, zm = device(x, y, (z + 1) % 8, c), device(x, y, (z + 7) % 8, c)
    yp, ym = device(x, (y + 1) % 8, z, c), device(x, (y + 7) % 8, z, c)
    yp2, ym2 = device(x, (y + 2) % 8, z, c), device(x, (y + 6) % 8, z, c)
    core = device(x, y, z, 1 - c)
    xk = {k: device((x + k) % 4, y, z, c) for k in (1, 2, 3)}

    barrier = pltpu.get_barrier_semaphore()
    partners = [zp, zm, yp, ym, yp2, ym2, core, xk[1], xk[2], xk[3]]
    for p in partners:
        pl.semaphore_signal(barrier, inc=1, device_id=p, device_id_type=MESH)

    taken, outgoing = [0], []

    def group(kind=0):
        taken[0] += 1
        return [taken[0] - 1, 0, kind]

    def send(src, dst_, where, into, units):
        out = outgoing[-1] if outgoing else None
        if into[2]:
            out = id_sent
        elif out is None or out[1] + units > UNITS:
            out = group()
            outgoing.append(out)
        pltpu.make_async_remote_copy(
            src_ref=src, dst_ref=dst_, send_sem=sems.at[out[0]], recv_sem=sems.at[into[0]],
            device_id=where, device_id_type=MESH,
        ).start()
        out[1] += units
        into[1] += units

    def wait(done, arrived):
        whole = (ids if done[2] else ar_).at[pl.ds(0, done[1])]
        copy = pltpu.make_async_remote_copy(
            src_ref=whole, dst_ref=whole, send_sem=sems.at[done[0]], recv_sem=sems.at[done[0]],
            device_id=core, device_id_type=MESH,
        )
        copy.wait_recv() if arrived else copy.wait_send()

    def arrive(*groups):
        for g in groups:
            wait(g, True)

    id_sent = group(1)

    live = lax.broadcasted_iota(jnp.int32, (cap, 1), 0) < cnt_ref[0]
    image_unit, image_inv = unit_rows(img_ref[...])
    img[0, 0] = jnp.where(live, image_unit, 0.0).astype(BF16)
    lane = lax.broadcasted_iota(jnp.int32, (8, 128), 1)
    slot = jnp.where(lane < cap, lane, lane - cap)
    id_own[...] = jnp.where(slot < cnt_ref[0], jnp.broadcast_to(own_ref[...], (8, 128)), -2)
    text_unit, text_inv = unit_rows(text_ref[...])
    tu[...] = jnp.zeros_like(tu)
    tu[0:pairs] = text_unit
    txt[0, 0, 0] = tu[0:16].astype(BF16)
    txt[1, 0, 0] = tu[16:32].astype(BF16)

    pl.semaphore_wait(barrier, len(partners))

    def hops_of(side, q):
        return 4 if q // 2 == side else 3

    def z_hop(h, side, q, into):
        rows, sign = pl.ds(16 * q, 16), 1 - 2 * side
        send(
            img.at[pos(sign * (1 - h)), 0, rows], img.at[pos(-sign * h), 0, rows], (zp, zm)[side],
            into, 1,
        )

    def a_hop(h, side, q, into):
        sign = 1 - 2 * side
        src, to = txt.at[0, pos(sign * (1 - h)), q], txt.at[0, pos(-sign * h), q]
        send(src, to, (yp, ym)[side], into, 1)

    def id_hop(h):
        into = group(1)
        send(ids.at[pos(1 - h)], ids.at[pos(-h)], zp, into, 1)
        if h < 4:
            send(ids.at[pos(h - 1)], ids.at[pos(h)], zm, into, 1)
        return into

    def core_pass(first, n):
        into, span = group(), pl.ds(first, n)
        send(img.at[span, 0], img.at[span, 1], core, into, 4 * n)
        return into

    def b_copy(source, distance, into):
        where = {1: yp, -1: ym, 2: yp2, -2: ym2}[distance]
        send(txt.at[1, pos(source), 0], txt.at[1, pos(source - distance), 0], where, into, 1)

    def b_across(first, n):
        into, span = group(), pl.ds(first, n)
        for k in (1, 2, 3):
            send(txt.at[1, span, 0], txt.at[1, span, 4 - k], xk[k], into, n)
        return into

    scale = scale_ref[0]
    bias = bias_ref[0]

    def score(half, gt, gi):
        texts = txt[half, 2 * gt : 2 * gt + 2].reshape(128, width)
        images = img[2 * gi : 2 * gi + 2].reshape(4 * cap, width)
        raw = lax.dot_general(
            texts, images, (((1,), (1,)), ((), ())), preferred_element_type=F32
        )
        e = jnp.exp(-(scale * raw + bias))
        slope = 1.0 / (1.0 + e)
        if gt in (0, 3):
            at = 0 if gt == 0 else 64
            half_y = y // 4 if gt == 0 else 1 - y // 4
            owner = half_y * 16 + z * 2 + c
            row = lax.broadcasted_iota(jnp.int32, (128, 1), 0) - at
            named = (row >= 0) & (row < 16) & (row + 16 * half < pairs)
            row_id = jnp.where(named, owner * pairs + 16 * half + row, -1)
            column_id = jnp.concatenate([ids[2 * gi, 0:1], ids[2 * gi + 1, 0:1]], axis=1)
            slope = jnp.where(row_id == column_id, -e * slope, slope)
        dst[
            half * 512 + gt * 128 : half * 512 + gt * 128 + 128, gi * 256 : gi * 256 + 256
        ] = (scale * slope).astype(BF16)

    def scores(s):
        for gi in range(s + 1):
            for half in (0, 1):
                score(half, s, gi)
        for gt in range(s):
            for half in (0, 1):
                score(half, gt, s)

    both = (0, 1)
    chunks = range(4)
    order = (0, 3, 1, 2)
    ax = {}
    for k in (1, 2, 3):
        ax[4 - k] = group()
        send(txt.at[0, 0, 0], txt.at[0, 0, 4 - k], xk[k], ax[4 - k], 1)
    bw = group()
    for d in (1, -1, 2, -2):
        b_copy(0, d, bw)
    waits = {}

    def start(flow, h, q):
        hop = (z_hop, a_hop)[flow]
        for side in both:
            if h <= hops_of(side, q):
                key = (flow, h, q if h < 4 else min(q, 3 - q))
                if key not in waits:
                    waits[key] = group()
                hop(h, side, q, waits[key])

    for q in order:
        start(0, 1, q)
    start(1, 1, 0)
    idw = group(1)
    send(id_own, id_sib, core, idw, 1)
    bx = {0: b_across(0, 1)}
    cw = {0: core_pass(0, 1)}
    for q in (3, 1, 2):
        arrive(ax[q])
        start(1, 1, q)
    arrive(idw)
    ids[0] = jnp.where(lane < cap, id_own[...], id_sib[...])
    idw = id_hop(1)
    spans = ((0, 1), (1, 2), (3, 2), (5, 2), (7, 1))

    def forward(flow, h):
        if h < 4:
            for q in order:
                arrive(waits[flow, h, q])
                start(flow, h + 1, q)
        else:
            arrive(waits[flow, 4, 0], waits[flow, 4, 1])
        if flow == 0:
            cw[h] = core_pass(*spans[h])

    forward(0, 1)
    arrive(bw)
    bw = group()
    for source, d in ((-2, 1), (2, -1), (-2, 2)):
        b_copy(source, d, bw)
    bx[1] = b_across(1, 4)
    arrive(idw)
    idw = id_hop(2)
    forward(1, 1)
    forward(0, 2)
    arrive(bw)
    bx[2] = b_across(5, 3)
    arrive(idw)
    idw = id_hop(3)
    forward(1, 2)
    arrive(cw[0], cw[1], bx[0], bx[1])
    scores(0)
    forward(0, 3)
    arrive(idw)
    idw = id_hop(4)
    forward(1, 3)
    arrive(cw[2])
    scores(1)
    forward(0, 4)
    arrive(idw)
    arrive(cw[3], bx[2])
    scores(2)
    forward(1, 4)
    arrive(cw[4])
    scores(3)

    def image_part(gi):
        g = lax.dot_general(
            dst[:, gi * 256 : gi * 256 + 256], txt[...].reshape(1024, width),
            (((0,), (0,)), ((), ())), preferred_element_type=F32,
        ).reshape(2, 2, cap, width)
        gown[2 * gi : 2 * gi + 2] = g[:, 0]
        gsend[2 * gi : 2 * gi + 2] = g[:, 1].astype(BF16)
        into, two = group(), pl.ds(2 * gi, 2)
        send(gsend.at[two], grecv.at[two], core, into, 8)
        return into

    def text_part(half, gt):
        images = img[...].reshape(16 * cap, width)
        t = jnp.dot(
            dst[half * 512 + gt * 128 : half * 512 + gt * 128 + 128, :], images,
            preferred_element_type=F32,
        )
        if half == 0:
            ta[2 * gt : 2 * gt + 2] = t.reshape(2, 64, width)
            return None
        t = t.reshape(2, 4, 16, width)
        tb[2 * gt : 2 * gt + 2] = t[:, 0]
        bxs[2 * gt : 2 * gt + 2] = t[:, 1:].astype(BF16)
        into, two = group(), pl.ds(2 * gt, 2)
        for k in (1, 2, 3):
            send(bxs.at[two, k - 1], bxr.at[two, k - 1], xk[k], into, 2)
        return into

    def image_sum(p, q):
        rows = pl.ds(16 * q, 16)
        return gown[p, rows] + grecv[p, rows].astype(F32)

    def a_sum(p, q):
        return ta[p, pl.ds(16 * q, 16)]

    def at(side, h, q):
        return (side * 4 + h - 1) * 4 + q

    def hop_back(flow, h, q):
        own, outs, ins, ends = flows[flow]
        key = (flow, h, q if h > 1 else min(q, 3 - q))
        if h == 2 and q in (0, 1):
            arrive(waits[flow, 1, q])
        if h > 2:
            arrive(waits[flow, h - 1, q])
        if key not in waits:
            waits[key] = group()
        for side in both:
            if h > 4 - hops_of(side, q):
                value = own(pos((1 - 2 * side) * (5 - h)), q)
                if h - 1 > 4 - hops_of(side, q):
                    value = value + ins[at(side, h - 1, q)].astype(F32)
                spot = at(side, h, q)
                outs[spot] = value.astype(BF16)
                send(outs.at[spot], ins.at[spot], ends[side], waits[key], 1)

    def ring_total(flow, q):
        own, _, ins, _ = flows[flow]
        arrive(waits[flow, 4, q])
        return own(0, q) + ins[at(0, 4, q)].astype(F32) + ins[at(1, 4, q)].astype(F32)

    def b_sum(p):
        return tb[p] + bxr[p, 0].astype(F32) + bxr[p, 1].astype(F32) + bxr[p, 2].astype(F32)

    def b_back(slot, value, where, into):
        bys[slot] = value.astype(BF16)
        send(bys.at[slot], byr.at[slot], where, into, 1)

    def came(slot):
        return byr[slot].astype(F32)

    flows = ((image_sum, zs, zr_, (zp, zm)), (a_sum, as_, ar_, (yp, ym)))
    waits = {}
    cores, across = {}, {}
    for h in (1, 2, 3, 4):
        g = 4 - h
        cores[g] = image_part(g)
        text_part(0, g)
        across[g] = text_part(1, g)
        for q in order:
            hop_back(1, h, q)
        arrive(cores[g])
        for q in order:
            hop_back(0, h, q)
        if h == 2:
            arrive(across[3], across[2])
            far = group()
            b_back(0, b_sum(pos(-3)), ym, far)
            b_back(1, b_sum(pos(4)), ym2, far)
            b_back(2, b_sum(pos(3)), yp, far)
    axw = group()
    own_a = None
    for q in order:
        value = ring_total(1, q)
        if q == 0:
            own_a = value
        else:
            axs[q - 1] = value.astype(BF16)
            send(axs.at[q - 1], axr.at[q - 1], xk[q], axw, 1)
    arrive(across[1], across[0], far)
    near = group()
    b_back(3, b_sum(pos(-2)) + came(0) + came(1), ym2, near)
    b_back(4, b_sum(pos(2)) + came(2), yp2, near)
    b_back(5, b_sum(pos(-1)), ym, near)
    b_back(6, b_sum(pos(1)), yp, near)
    total = jnp.concatenate([ring_total(0, q) for q in chunks])
    ig_ref[...] = jnp.where(live, unit_back(total, image_unit, image_inv), 0.0)
    arrive(axw)
    total_a = own_a
    for k in range(3):
        total_a = total_a + axr[k].astype(F32)
    arrive(near)
    total_b = b_sum(0) + came(3) + came(4) + came(5) + came(6)
    total = jnp.concatenate([total_a, total_b])[0:pairs]
    tg_ref[...] = unit_back(total, tu[0:pairs], text_inv)
    for g in outgoing + [id_sent]:
        wait(g, False)


def shards(tower_images, owners, counts, text, logit_scale, logit_bias):
    cap, width = tower_images.shape
    pairs = text.shape[0]
    twice = jnp.concatenate([owners, owners]).reshape(1, 2 * cap)
    vmem = pl.BlockSpec(memory_space=pltpu.VMEM)
    smem = pl.BlockSpec(memory_space=pltpu.SMEM)
    V = pltpu.VMEM
    return pl.pallas_call(
        kernel,
        out_shape=(
            jax.ShapeDtypeStruct((cap, width), F32),
            jax.ShapeDtypeStruct((pairs, width), F32),
        ),
        in_specs=[vmem, vmem, smem, vmem, smem, smem],
        out_specs=(vmem, vmem),
        scratch_shapes=[
            V((8, 2, cap, width), BF16),
            V((8, 8, 128), jnp.int32),
            V((8, 128), jnp.int32),
            V((8, 128), jnp.int32),
            V((2, 8, 4, 16, width), BF16),
            V((1024, 1024), BF16),
            V((32, width), F32),
            V((8, cap, width), F32),
            V((8, cap, width), BF16),
            V((8, cap, width), BF16),
            V((32, 16, width), BF16),
            V((32, 16, width), BF16),
            V((8, 64, width), F32),
            V((32, 16, width), BF16),
            V((32, 16, width), BF16),
            V((3, 16, width), BF16),
            V((3, 16, width), BF16),
            V((8, 16, width), F32),
            V((8, 3, 16, width), BF16),
            V((8, 3, 16, width), BF16),
            V((7, 16, width), BF16),
            V((7, 16, width), BF16),
            pltpu.SemaphoreType.DMA((SEMAPHORES,)),
        ],
        compiler_params=pltpu.CompilerParams(
            collective_id=0, has_side_effects=True, vmem_limit_bytes=56 << 20
        ),
    )(tower_images, twice, counts, text, logit_scale, logit_bias)


def solution(mesh):
    split = P(("blk", "grp"))
    rows = P(("blk", "grp"), None)
    return jax.shard_map(
        shards, mesh=mesh, in_specs=(rows, split, split, rows, P(), P()), out_specs=(rows, rows),
        check_vma=False,
    )
```

time: 85.3 us -> 71.8 us (0.84)
  the two profiles are of different devices: /device:TPU:24 before, /device:TPU:1 now
where the time goes in v2:
time: 71.8 us; the launch traced here: 71.6 us
  Pallas kernels  66 us (92%)
  between operations  2.62 us (4%)
  local copies, waits for them, and re-layouts  2.4 us (3%)
    pallas_call x1, Pallas kernels, shards(): pl.pallas_call(kernel, out_shape=(jax.ShapeDtypeStruct((cap, width), F32)...  66 us
    unnamed x6, local copies, waits for them, and re-layouts  2.4 us

profile of v2, /device:TPU:1, one launch (start us, length us, event | category | flops | bytes accessed | tf_op | source)
XLA Modules:
  0.0 71.6 jit_solution(17680895768834379715)
XLA Ops:
  1.9 0.0 copy-start.1
  2.6 0.0 copy-done.1
  2.6 0.6 add_bitcast_fusion.own_ref
  3.2 66.0 %shard_map.77 = (f32[64,1152]{1,0:T(8,128)}, f32[28,1152]{1,0:T(8,128)}) custom-call(bf16[64,1152]{1,0:T(8,128)(2,1)} %img_ref.1, s32[1,128]{1,0:T(1,128)} %add_bitcast_fusion.own_ref, s32[1]{0:T(128)S(6)} %copy.10.cnt_ref, bf16[28,1152]{1,0:T(8,128)(2,1)} %text_ref.1, f32[1]{0:T(128)S(6)} %copy.11.scale_ref, f32[1]{0:T(128)S(6)} %copy.12.bias_ref), custom_call_target="tpu_custom_call" | custom-call | tf_op jit(solution)/shard_map/pallas_call | solution.py:379
  69.2 0.0 copy-start
  69.2 1.7 %copy.13 = f32[64,1152]{1,0:T(8,128)} copy(f32[64,1152]{1,0:T(8,128)} %get-tuple-element.4) | data formatting | bytes 589824
  70.9 0.0 copy-done
  70.9 0.7 copy.14
Async XLA Ops:
  1.9 0.7 copy-start.1
  69.2 1.7 %copy-start = (f32[28,1152]{1,0:T(8,128)S(1)}, f32[28,1152]{1,0:T(8,128)}, u32[]{:S(2)}) copy-start(f32[28,1152]{1,0:T(8,128)} %get-tuple-element.5) | copy-start | bytes 387076

commit v3 on v2

v3 whole, which is shorter than its diff:
```python
import jax
import jax.numpy as jnp
from jax import lax
from jax.experimental import pallas as pl
from jax.experimental.pallas import tpu as pltpu
from jax.sharding import PartitionSpec as P

MESH = pl.DeviceIdType.MESH
F32 = jnp.float32
BF16 = jnp.bfloat16
ORDER = (0, 1, -1, 2, -2, 3, -3, 4)
UNITS = 32
PACKED = 896
BASE = (16, 0)
SEMAPHORES = 108


def pos(offset):
    return ORDER.index(4 if offset == -4 else offset)


def unit_rows(values):
    wide = values.astype(F32)
    inverse = lax.rsqrt(jnp.sum(wide * wide, axis=-1, keepdims=True) + 1e-06)
    return wide * inverse, inverse


def unit_back(grad, unit, inverse):
    return (grad - unit * jnp.sum(unit * grad, axis=-1, keepdims=True)) * inverse


def pack(rows):
    low = lax.broadcasted_iota(jnp.int32, (8, 128), 0) < 4
    spare = []
    for tile in (7, 8):
        lanes = slice(128 * tile, 128 * tile + 128)
        up, down = rows[0:8, lanes], rows[8:16, lanes]
        spare += [pltpu.roll(up, 4, 0), up, pltpu.roll(down, 4, 0)]
    spare.append(jnp.zeros((8, 128), F32))
    second = [
        jnp.where(low, rows[8:16, 128 * m : 128 * m + 128], spare[m]) for m in range(7)
    ]
    return jnp.concatenate([rows[0:8, 0:PACKED], jnp.concatenate(second, axis=1)], axis=0)


def unpack(rows):
    low = lax.broadcasted_iota(jnp.int32, (8, 128), 0) < 4
    zero = jnp.zeros((8, 128), F32)
    part = [rows[8:16, 128 * m : 128 * m + 128] for m in range(7)]
    up, down = [rows[0:8]], [jnp.where(low, p, zero) for p in part]
    for m in (0, 3):
        up.append(jnp.where(low, pltpu.roll(part[m], 4, 0), part[m + 1]))
        down.append(jnp.where(low, pltpu.roll(part[m + 2], 4, 0), zero))
    return jnp.concatenate([jnp.concatenate(up, axis=1), jnp.concatenate(down, axis=1)], axis=0)


def kernel(
    img_ref, own_ref, cnt_ref, text_ref, scale_ref, bias_ref,
    ig_ref, tg_ref,
    img, ids, id_own, id_sib, txt, pk, dst, tu,
    gown, gsend, grecv, zs, zr_, ta, as_, ar_, axs, axr, tb, bxs, bxr, bys, byr,
    sems,
):
    width = img_ref.shape[1]
    cap = img_ref.shape[0]
    pairs = text_ref.shape[0]
    blk = lax.axis_index("blk")
    grp = lax.axis_index("grp")
    x, y = blk % 4, (grp // 16) * 4 + blk // 4
    z, c = (grp // 2) % 8, grp % 2

    def device(x, y, z, c):
        return ((y % 4) * 4 + x, (y // 4) * 16 + z * 2 + c)

    zp, zm = device(x, y, (z + 1) % 8, c), device(x, y, (z + 7) % 8, c)
    yp, ym = device(x, (y + 1) % 8, z, c), device(x, (y + 7) % 8, z, c)
    yp2, ym2 = device(x, (y + 2) % 8, z, c), device(x, (y + 6) % 8, z, c)
    core = device(x, y, z, 1 - c)
    xk = {k: device((x + k) % 4, y, z, c) for k in (1, 2, 3)}

    barrier = pltpu.get_barrier_semaphore()
    partners = [zp, zm, yp, ym, yp2, ym2, core, xk[1], xk[2], xk[3]]
    for p in partners:
        pl.semaphore_signal(barrier, inc=1, device_id=p, device_id_type=MESH)

    taken, outgoing = [0], []
    full = {0: zr_, 1: ids, 2: pk}

    def group(kind=0):
        taken[0] += 1
        return [taken[0] - 1, 0, kind]

    def send(src, dst_, where, into, units):
        same = [g for g in outgoing if g[2] == into[2]]
        if same and same[-1][1] + units <= UNITS:
            out = same[-1]
        else:
            out = group(into[2])
            outgoing.append(out)
        pltpu.make_async_remote_copy(
            src_ref=src, dst_ref=dst_, send_sem=sems.at[out[0]], recv_sem=sems.at[into[0]],
            device_id=where, device_id_type=MESH,
        ).start()
        out[1] += units
        into[1] += units

    def wait(done, arrived):
        whole = full[done[2]].at[pl.ds(0, int(done[1]))]
        copy = pltpu.make_async_remote_copy(
            src_ref=whole, dst_ref=whole, send_sem=sems.at[done[0]], recv_sem=sems.at[done[0]],
            device_id=core, device_id_type=MESH,
        )
        copy.wait_recv() if arrived else copy.wait_send()

    def arrive(*groups):
        for g in groups:
            wait(g, True)

    live = lax.broadcasted_iota(jnp.int32, (cap, 1), 0) < cnt_ref[0]
    image_unit, image_inv = unit_rows(img_ref[...])
    img[0, 0] = jnp.where(live, image_unit, 0.0).astype(BF16)
    lane = lax.broadcasted_iota(jnp.int32, (8, 128), 1)
    slot = jnp.where(lane < cap, lane, lane - cap)
    id_own[...] = jnp.zeros_like(id_own)
    id_own[:, 0:cap] = jnp.broadcast_to(own_ref[...], (8, cap))
    twice = jnp.where(lane < cap, id_own[...], pltpu.roll(id_own[...], cap, 1))
    id_own[...] = jnp.where(slot < cnt_ref[0], twice, -2)
    text_unit, text_inv = unit_rows(text_ref[...])
    tu[...] = jnp.zeros_like(tu)
    tu[0:pairs] = text_unit
    txt[1, 0, 0] = tu[0:16].astype(BF16)
    pk[0] = pack(tu[16:32]).astype(BF16)

    pl.semaphore_wait(barrier, len(partners))

    both = (0, 1)
    cut = 128 * ((width // 128 + 1) // 2)
    left, right = pl.ds(0, cut), pl.ds(cut, width - cut)

    def hops_of(side, q):
        return 4 if q // 2 == side else 3

    def z_hop(h, side, q, into):
        rows, sign = pl.ds(16 * q, 16), 1 - 2 * side
        send(
            img.at[pos(sign * (1 - h)), 0, rows], img.at[pos(-sign * h), 0, rows], (zp, zm)[side],
            into, 1,
        )

    def a_hop(h, side, q, into):
        sign = 1 - 2 * side
        src, to = pk.at[4 * pos(sign * (1 - h)) + q], pk.at[4 * pos(-sign * h) + q]
        send(src, to, (yp, ym)[side], into, 1)

    def id_hop(h):
        into = group(1)
        send(ids.at[pos(1 - h)], ids.at[pos(-h)], zp, into, 1)
        if h < 4:
            send(ids.at[pos(h - 1)], ids.at[pos(h)], zm, into, 1)
        return into

    def core_pass(first, n):
        into, span = group(), pl.ds(first, n)
        send(img.at[span, 0], img.at[span, 1], core, into, 4 * n)
        return into

    def b_hop(h):
        into = group()
        if h < 4:
            send(txt.at[1, pos(1 - h), 0], txt.at[1, pos(-h), 0], yp, into, 1)
            send(txt.at[1, pos(h - 1), 0], txt.at[1, pos(h), 0], ym, into, 1)
        else:
            for source, where, lanes in ((-3, yp, left), (3, ym, right)):
                send(txt.at[1, pos(source), 0, :, lanes], txt.at[1, 7, 0, :, lanes], where, into, 0.5)
        return into

    def b_across(first, n, far):
        into, span = group(), pl.ds(first, n)
        for k in (1, 3) + ((2,) if far else ()):
            send(txt.at[1, span, 0], txt.at[1, span, 4 - k], xk[k], into, n)
        return into

    def b_onward(first, n):
        into, span = group(), pl.ds(first, n)
        for source, k, lanes in ((3, 1, left), (1, 3, right)):
            send(
                txt.at[1, span, source, :, lanes], txt.at[1, span, 2, :, lanes], xk[k], into, n / 2
            )
        return into

    scale = scale_ref[0]
    bias = bias_ref[0]

    def score(half, gt, gi):
        texts = txt[half, 2 * gt : 2 * gt + 2].reshape(128, width)
        images = img[2 * gi : 2 * gi + 2].reshape(4 * cap, width)
        raw = lax.dot_general(
            texts, images, (((1,), (1,)), ((), ())), preferred_element_type=F32
        )
        e = jnp.exp(-(scale * raw + bias))
        slope = 1.0 / (1.0 + e)
        if gt in (0, 3):
            at = 0 if gt == 0 else 64
            half_y = y // 4 if gt == 0 else 1 - y // 4
            owner = half_y * 16 + z * 2 + c
            row = lax.broadcasted_iota(jnp.int32, (128, 1), 0) - at
            named = (row >= 0) & (row < 16) & (row + BASE[half] < pairs)
            row_id = jnp.where(named, owner * pairs + BASE[half] + row, -1)
            column_id = jnp.concatenate([ids[2 * gi, 0:1], ids[2 * gi + 1, 0:1]], axis=1)
            slope = jnp.where(row_id == column_id, -e * slope, slope)
        dst[
            half * 512 + gt * 128 : half * 512 + gt * 128 + 128, gi * 256 : gi * 256 + 256
        ] = (scale * slope).astype(BF16)

    def scores(tiles):
        for half, gt, gi in tiles:
            score(half, gt, gi)

    def known(s):
        return [(half, s, gi) for gi in range(s + 1) for half in both] + [
            (half, gt, s) for gt in range(s) for half in both
        ]

    chunks = range(4)
    order = (0, 3, 1, 2)
    ax = {}
    for k in (1, 2, 3):
        ax[4 - k] = group(2)
        send(pk.at[0], pk.at[4 - k], xk[k], ax[4 - k], 1)
    bw = b_hop(1)
    waits = {}

    def start(flow, h, q):
        hop = (z_hop, a_hop)[flow]
        for side in both:
            if h <= hops_of(side, q):
                key = (flow, h, q if h < 4 else min(q, 3 - q))
                if key not in waits:
                    waits[key] = group(2 * flow)
                hop(h, side, q, waits[key])

    for q in order:
        start(0, 1, q)
    start(1, 1, 0)
    idw = group(1)
    send(id_own, id_sib, core, idw, 1)
    bx = {0: b_across(0, 1, False)}
    by = {}
    cw = {0: core_pass(0, 1)}
    for q in (3, 1, 2):
        arrive(ax[q])
        start(1, 1, q)
    arrive(idw)
    ids[0] = jnp.where(lane < cap, id_own[...], id_sib[...])
    idw = id_hop(1)
    spans = ((0, 1), (1, 2), (3, 2), (5, 2), (7, 1))

    def spread(p):
        for k in chunks:
            txt[0, p, k] = unpack(pk[4 * p + k].astype(F32)).astype(BF16)

    def onward(h):
        arrive(bx[h])
        by[h] = b_onward(*spans[h])

    def forward(flow, h):
        if h < 4:
            for q in order:
                arrive(waits[flow, h, q])
                start(flow, h + 1, q)
        else:
            arrive(waits[flow, 4, 0], waits[flow, 4, 1])
        if flow == 0:
            cw[h] = core_pass(*spans[h])
        else:
            for p in (pos(h), pos(-h)) if h < 4 else (7,):
                spread(p)

    def b_forward(h):
        arrive(bw_[0])
        if h < 4:
            bw_[0] = b_hop(h + 1)
        bx[h] = b_across(*spans[h], h > 2)

    bw_ = [bw]
    b_forward(1)
    onward(0)
    spread(0)
    forward(0, 1)
    arrive(idw)
    idw = id_hop(2)
    forward(1, 1)
    onward(1)
    b_forward(2)
    forward(0, 2)
    arrive(idw)
    idw = id_hop(3)
    forward(1, 2)
    onward(2)
    b_forward(3)
    arrive(cw[0], cw[1], by[0], by[1])
    scores(known(0))
    forward(0, 3)
    arrive(idw)
    idw = id_hop(4)
    forward(1, 3)
    b_forward(4)
    arrive(cw[2], by[2])
    scores(known(1))
    forward(0, 4)
    arrive(idw)
    arrive(cw[3], bx[3])
    scores(known(2))
    arrive(cw[4], bx[4])
    last = known(3)
    scores([t for t in last if t[:2] != (0, 3)])
    forward(1, 4)
    scores([t for t in last if t[:2] == (0, 3)])

    def image_part(gi):
        g = lax.dot_general(
            dst[:, gi * 256 : gi * 256 + 256], txt[...].reshape(1024, width),
            (((0,), (0,)), ((), ())), preferred_element_type=F32,
        ).reshape(2, 2, cap, width)
        gown[2 * gi : 2 * gi + 2] = g[:, 0]
        gsend[2 * gi : 2 * gi + 2] = g[:, 1].astype(BF16)
        into, two = group(), pl.ds(2 * gi, 2)
        send(gsend.at[two], grecv.at[two], core, into, 8)
        return into

    def text_part(half, gt):
        images = img[...].reshape(16 * cap, width)
        t = jnp.dot(
            dst[half * 512 + gt * 128 : half * 512 + gt * 128 + 128, :], images,
            preferred_element_type=F32,
        )
        if half == 0:
            for m in range(8):
                ta[8 * gt + m] = pack(t[16 * m : 16 * m + 16])
            return None
        t = t.reshape(2, 4, 16, width)
        tb[2 * gt : 2 * gt + 2] = t[:, 0]
        bxs[2 * gt : 2 * gt + 2] = t[:, 1:].astype(BF16)
        into, two = group(), pl.ds(2 * gt, 2)
        for k in (1, 2, 3):
            send(bxs.at[two, k - 1], bxr.at[two, k - 1], xk[k], into, 2)
        return into

    def image_sum(p, q):
        rows = pl.ds(16 * q, 16)
        return gown[p, rows] + grecv[p, rows].astype(F32)

    def a_sum(p, q):
        return ta[4 * p + q]

    def at(side, h, q):
        return (side * 4 + h - 1) * 4 + q

    def hop_back(flow, h, side, q):
        own, outs, ins, ends = flows[flow]
        first = 5 - hops_of(side, q)
        if h < first:
            return
        key = (flow, h, q if h > 1 else min(q, 3 - q))
        if key not in waits:
            waits[key] = group(2 * flow)
        value = own(pos((1 - 2 * side) * (5 - h)), q)
        if h > first:
            value = value + ins[at(side, h - 1, q)].astype(F32)
        spot = at(side, h, q)
        outs[spot] = value.astype(BF16)
        send(outs.at[spot], ins.at[spot], ends[side], waits[key], 1)

    def begin(flow, h):
        for q in order:
            for side in both:
                if 5 - hops_of(side, q) == h:
                    hop_back(flow, h, side, q)

    def carry(flow, h):
        for q in order:
            if h == 2:
                if q in (0, 1):
                    arrive(waits[flow, 1, q])
                hop_back(flow, 2, q // 2, q)
            else:
                arrive(waits[flow, h - 1, q])
                for side in both:
                    hop_back(flow, h, side, q)

    def ring_total(flow, q):
        own, _, ins, _ = flows[flow]
        arrive(waits[flow, 4, q])
        return own(0, q) + ins[at(0, 4, q)].astype(F32) + ins[at(1, 4, q)].astype(F32)

    def b_sum(p):
        return tb[p] + bxr[p, 0].astype(F32) + bxr[p, 1].astype(F32) + bxr[p, 2].astype(F32)

    def b_back(slot, value, where, into):
        bys[slot] = value.astype(BF16)
        send(bys.at[slot], byr.at[slot], where, into, 1)

    def b_far():
        far = group()
        b_back(0, b_sum(pos(-3)), ym, far)
        b_back(2, b_sum(pos(3)), yp, far)
        bys[1] = b_sum(pos(4)).astype(BF16)
        for where, lanes in ((ym2, left), (yp2, right)):
            send(bys.at[1, :, lanes], byr.at[1, :, lanes], where, far, 0.5)
        return far

    def came(slot):
        return byr[slot].astype(F32)

    leftish = lax.broadcasted_iota(jnp.int32, (16, width), 1) < cut
    flows = ((image_sum, zs, zr_, (zp, zm)), (a_sum, as_, ar_, (yp, ym)))
    waits = {}
    cores, across = {}, {}
    text_part(0, 3)
    begin(1, 1)
    cores[3] = image_part(3)
    across[3] = text_part(1, 3)
    text_part(0, 2)
    begin(1, 2)
    cores[2] = image_part(2)
    arrive(cores[3])
    begin(0, 1)
    across[2] = text_part(1, 2)
    arrive(cores[2])
    begin(0, 2)
    carry(1, 2)
    text_part(0, 1)
    across[1] = text_part(1, 1)
    cores[1] = image_part(1)
    carry(0, 2)
    text_part(0, 0)
    across[0] = text_part(1, 0)
    carry(1, 3)
    arrive(cores[1])
    cores[0] = image_part(0)
    carry(0, 3)
    arrive(across[3], across[2])
    far = b_far()
    carry(1, 4)
    arrive(cores[0])
    carry(0, 4)
    arrive(across[1], across[0], far)
    near = group()
    wide = came(1)
    zeros = jnp.zeros((16, width), F32)
    b_back(3, b_sum(pos(-2)) + came(0) + jnp.where(leftish, wide, zeros), ym2, near)
    b_back(4, b_sum(pos(2)) + came(2) + jnp.where(leftish, zeros, wide), yp2, near)
    b_back(5, b_sum(pos(-1)), ym, near)
    b_back(6, b_sum(pos(1)), yp, near)
    axw = group(2)
    own_a = None
    for q in order:
        value = ring_total(1, q)
        if q == 0:
            own_a = value
        else:
            axs[q - 1] = value.astype(BF16)
            send(axs.at[q - 1], axr.at[q - 1], xk[q], axw, 1)
    total = jnp.concatenate([ring_total(0, q) for q in chunks])
    ig_ref[...] = jnp.where(live, unit_back(total, image_unit, image_inv), 0.0)
    arrive(axw)
    total_a = own_a
    for k in range(3):
        total_a = total_a + axr[k].astype(F32)
    arrive(near)
    total_b = b_sum(0) + came(3) + came(4) + came(5) + came(6)
    total = jnp.concatenate([total_b, unpack(total_a)])[0:pairs]
    tg_ref[...] = unit_back(total, tu[0:pairs], text_inv)
    for g in outgoing:
        wait(g, False)


def hand_out(a_ref, b_ref, c_ref, d_ref):
    c_ref[...] = a_ref[...]
    d_ref[...] = b_ref[...]


def shards(tower_images, owners, counts, text, logit_scale, logit_bias):
    cap, width = tower_images.shape
    pairs = text.shape[0]
    vmem = pl.BlockSpec(memory_space=pltpu.VMEM)
    smem = pl.BlockSpec(memory_space=pltpu.SMEM)
    V = pltpu.VMEM
    grads = pl.pallas_call(
        kernel,
        out_shape=(
            jax.ShapeDtypeStruct((cap, width), F32),
            jax.ShapeDtypeStruct((pairs, width), F32),
        ),
        in_specs=[vmem, vmem, smem, vmem, smem, smem],
        out_specs=(vmem, vmem),
        scratch_shapes=[
            V((8, 2, cap, width), BF16),
            V((8, 8, 128), jnp.int32),
            V((8, 128), jnp.int32),
            V((8, 128), jnp.int32),
            V((2, 8, 4, 16, width), BF16),
            V((32, 16, PACKED), BF16),
            V((1024, 1024), BF16),
            V((32, width), F32),
            V((8, cap, width), F32),
            V((8, cap, width), BF16),
            V((8, cap, width), BF16),
            V((32, 16, width), BF16),
            V((32, 16, width), BF16),
            V((32, 16, PACKED), F32),
            V((32, 16, PACKED), BF16),
            V((32, 16, PACKED), BF16),
            V((3, 16, PACKED), BF16),
            V((3, 16, PACKED), BF16),
            V((8, 16, width), F32),
            V((8, 3, 16, width), BF16),
            V((8, 3, 16, width), BF16),
            V((7, 16, width), BF16),
            V((7, 16, width), BF16),
            pltpu.SemaphoreType.DMA((SEMAPHORES,)),
        ],
        compiler_params=pltpu.CompilerParams(
            collective_id=0, has_side_effects=True, vmem_limit_bytes=56 << 20
        ),
    )(tower_images, owners.reshape(1, cap), counts, text, logit_scale, logit_bias)
    return pl.pallas_call(
        hand_out,
        out_shape=tuple(jax.ShapeDtypeStruct(g.shape, g.dtype) for g in grads),
        in_specs=[vmem, vmem],
        out_specs=(vmem, vmem),
    )(*grads)


def solution(mesh):
    split = P(("blk", "grp"))
    rows = P(("blk", "grp"), None)
    return jax.shard_map(
        shards, mesh=mesh, in_specs=(rows, split, split, rows, P(), P()), out_specs=(rows, rows),
        check_vma=False,
    )
```

time: 71.8 us -> 66.2 us (0.922)
  Pallas kernels: 66 us -> 63.5 us
  local copies, waits for them, and re-layouts: 2.4 us -> 0 us
    pallas_call x1, Pallas kernels: 66 us -> 61.7 us  [shards(): pl.pallas_call(kernel, out_shape=(jax.ShapeDtypeStruct((cap, width), F32)...]
    unnamed x6 -> x0, local copies, waits for them, and re-layouts: 2.4 us -> none
    pallas_call x0 -> x1, Pallas kernels: none -> 1.78 us  [shards(): pl.pallas_call(hand_out, out_shape=tuple((jax.ShapeDtypeStruct(g.shape, g...]
where the time goes in v3:
time: 66.2 us; the launch traced here: 66.1 us
  Pallas kernels  63.5 us (96%)
  between operations  2.58 us (4%)
    pallas_call x1, Pallas kernels, shards(): pl.pallas_call(kernel, out_shape=(jax.ShapeDtypeStruct((cap, width), F32)...  61.7 us
    pallas_call x1, Pallas kernels, shards(): pl.pallas_call(hand_out, out_shape=tuple((jax.ShapeDtypeStruct(g.shape, g...  1.78 us

profile of v3, /device:TPU:1, one launch (start us, length us, event | category | flops | bytes accessed | tf_op | source)
XLA Modules:
  0.0 66.1 jit_solution(16061890409072146920)
XLA Ops:
  2.6 61.7 %shard_map.77 = (f32[64,1152]{1,0:T(8,128)}, f32[28,1152]{1,0:T(8,128)}) custom-call(bf16[64,1152]{1,0:T(8,128)(2,1)} %img_ref.1, s32[1,64]{1,0:T(1,128)} %bitcast.1, s32[1]{0:T(128)S(6)} %copy.8.cnt_ref, bf16[28,1152]{1,0:T(8,128)(2,1)} %text_ref.1, f32[1]{0:T(128)S(6)} %copy.9.scale_ref, f32[1]{0:T(128)S(6)} %copy.10.bias_ref), custom_call_target="tpu_custom_call" | custom-call | tf_op jit(solution)/shard_map/pallas_call | solution.py:489
  64.3 1.8 %shard_map.78 = (f32[64,1152]{1,0:T(8,128)}, f32[28,1152]{1,0:T(8,128)}) custom-call(f32[64,1152]{1,0:T(8,128)} %get-tuple-element.4.a_ref, f32[28,1152]{1,0:T(8,128)} %get-tuple-element.5.b_ref), custom_call_target="tpu_custom_call" | custom-call | tf_op jit(solution)/shard_map/pallas_call | solution.py:527

commit v4 on v3

--- a/solution.py
+++ b/solution.py
@@ -12,7 +12,7 @@
 UNITS = 32
 PACKED = 896
 BASE = (16, 0)
-SEMAPHORES = 108
+SEMAPHORES = 112
 
 
 def pos(offset):
@@ -116,7 +116,7 @@
         for g in groups:
             wait(g, True)
 
-    live = lax.broadcasted_iota(jnp.int32, (cap, 1), 0) < cnt_ref[0]
+    live = lax.broadcasted_iota(jnp.int32, (cap, 1), 0) < cnt_ref[...]
     image_unit, image_inv = unit_rows(img_ref[...])
     img[0, 0] = jnp.where(live, image_unit, 0.0).astype(BF16)
     lane = lax.broadcasted_iota(jnp.int32, (8, 128), 1)
@@ -124,7 +124,7 @@
     id_own[...] = jnp.zeros_like(id_own)
     id_own[:, 0:cap] = jnp.broadcast_to(own_ref[...], (8, cap))
     twice = jnp.where(lane < cap, id_own[...], pltpu.roll(id_own[...], cap, 1))
-    id_own[...] = jnp.where(slot < cnt_ref[0], twice, -2)
+    id_own[...] = jnp.where(slot < cnt_ref[...], twice, -2)
     text_unit, text_inv = unit_rows(text_ref[...])
     tu[...] = jnp.zeros_like(tu)
     tu[0:pairs] = text_unit
@@ -166,33 +166,26 @@
 
     def b_hop(h):
         into = group()
-        if h < 4:
-            send(txt.at[1, pos(1 - h), 0], txt.at[1, pos(-h), 0], yp, into, 1)
-            send(txt.at[1, pos(h - 1), 0], txt.at[1, pos(h), 0], ym, into, 1)
-        else:
-            for source, where, lanes in ((-3, yp, left), (3, ym, right)):
-                send(txt.at[1, pos(source), 0, :, lanes], txt.at[1, 7, 0, :, lanes], where, into, 0.5)
+        send(txt.at[1, pos(1 - h), 0], txt.at[1, pos(-h), 0], yp, into, 1)
+        send(txt.at[1, pos(h - 1), 0], txt.at[1, pos(h), 0], ym, into, 1)
+        if h == 3:
+            for source, where, lanes in ((-2, yp2, left), (2, ym2, right)):
+                src, to = txt.at[1, pos(source), 0, :, lanes], txt.at[1, 7, 0, :, lanes]
+                send(src, to, where, into, 0.5)
         return into
 
-    def b_across(first, n, far):
+    def b_across(first, n):
         into, span = group(), pl.ds(first, n)
-        for k in (1, 3) + ((2,) if far else ()):
+        for k in (1, 2, 3):
             send(txt.at[1, span, 0], txt.at[1, span, 4 - k], xk[k], into, n)
         return into
 
-    def b_onward(first, n):
-        into, span = group(), pl.ds(first, n)
-        for source, k, lanes in ((3, 1, left), (1, 3, right)):
-            send(
-                txt.at[1, span, source, :, lanes], txt.at[1, span, 2, :, lanes], xk[k], into, n / 2
-            )
-        return into
-
-    scale = scale_ref[0]
-    bias = bias_ref[0]
-
-    def score(half, gt, gi):
-        texts = txt[half, 2 * gt : 2 * gt + 2].reshape(128, width)
+    scale = scale_ref[...]
+    bias = bias_ref[...]
+
+    def score(halves, gt, gi):
+        first, n = halves[0], len(halves)
+        texts = txt[first : first + n, 2 * gt : 2 * gt + 2].reshape(128 * n, width)
         images = img[2 * gi : 2 * gi + 2].reshape(4 * cap, width)
         raw = lax.dot_general(
             texts, images, (((1,), (1,)), ((), ())), preferred_element_type=F32
@@ -203,23 +196,25 @@
             at = 0 if gt == 0 else 64
             half_y = y // 4 if gt == 0 else 1 - y // 4
             owner = half_y * 16 + z * 2 + c
-            row = lax.broadcasted_iota(jnp.int32, (128, 1), 0) - at
-            named = (row >= 0) & (row < 16) & (row + BASE[half] < pairs)
-            row_id = jnp.where(named, owner * pairs + BASE[half] + row, -1)
+            row_ids = []
+            for half in halves:
+                row = lax.broadcasted_iota(jnp.int32, (128, 1), 0) - at
+                named = (row >= 0) & (row < 16) & (row + BASE[half] < pairs)
+                row_ids.append(jnp.where(named, owner * pairs + BASE[half] + row, -1))
+            row_id = jnp.concatenate(row_ids, axis=0)
             column_id = jnp.concatenate([ids[2 * gi, 0:1], ids[2 * gi + 1, 0:1]], axis=1)
             slope = jnp.where(row_id == column_id, -e * slope, slope)
-        dst[
-            half * 512 + gt * 128 : half * 512 + gt * 128 + 128, gi * 256 : gi * 256 + 256
-        ] = (scale * slope).astype(BF16)
+        d = (scale * slope).astype(BF16)
+        for k, half in enumerate(halves):
+            to = half * 512 + gt * 128
+            dst[to : to + 128, gi * 256 : gi * 256 + 256] = d[128 * k : 128 * k + 128]
 
     def scores(tiles):
-        for half, gt, gi in tiles:
-            score(half, gt, gi)
+        for halves, gt, gi in tiles:
+            score(halves, gt, gi)
 
     def known(s):
-        return [(half, s, gi) for gi in range(s + 1) for half in both] + [
-            (half, gt, s) for gt in range(s) for half in both
-        ]
+        return [(both, s, gi) for gi in range(s + 1)] + [(both, gt, s) for gt in range(s)]
 
     chunks = range(4)
     order = (0, 3, 1, 2)
@@ -244,8 +239,7 @@
     start(1, 1, 0)
     idw = group(1)
     send(id_own, id_sib, core, idw, 1)
-    bx = {0: b_across(0, 1, False)}
-    by = {}
+    bx = {0: b_across(0, 1)}
     cw = {0: core_pass(0, 1)}
     for q in (3, 1, 2):
         arrive(ax[q])
@@ -254,93 +248,98 @@
     ids[0] = jnp.where(lane < cap, id_own[...], id_sib[...])
     idw = id_hop(1)
     spans = ((0, 1), (1, 2), (3, 2), (5, 2), (7, 1))
+    b_spans = ((0, 1), (1, 2), (3, 2), (5, 3))
 
     def spread(p):
         for k in chunks:
             txt[0, p, k] = unpack(pk[4 * p + k].astype(F32)).astype(BF16)
-
-    def onward(h):
-        arrive(bx[h])
-        by[h] = b_onward(*spans[h])
 
     def forward(flow, h):
         if h < 4:
             for q in order:
                 arrive(waits[flow, h, q])
                 start(flow, h + 1, q)
+        elif flow == 1:
+            arrive(waits[flow, 4, 0], waits[flow, 4, 1])
         else:
-            arrive(waits[flow, 4, 0], waits[flow, 4, 1])
-        if flow == 0:
+            cw[4] = group()
+            for k in both:
+                arrive(waits[flow, 4, k])
+                for q in (k, 3 - k):
+                    rows = pl.ds(16 * q, 16)
+                    send(img.at[7, 0, rows], img.at[7, 1, rows], core, cw[4], 1)
+        if flow == 0 and h < 4:
             cw[h] = core_pass(*spans[h])
-        else:
-            for p in (pos(h), pos(-h)) if h < 4 else (7,):
-                spread(p)
+        elif flow == 1:
+            if h == 4:
+                spread(7)
 
     def b_forward(h):
         arrive(bw_[0])
-        if h < 4:
+        if h < 3:
             bw_[0] = b_hop(h + 1)
-        bx[h] = b_across(*spans[h], h > 2)
+        bx[h] = b_across(*b_spans[h])
 
     bw_ = [bw]
     b_forward(1)
-    onward(0)
-    spread(0)
     forward(0, 1)
     arrive(idw)
     idw = id_hop(2)
     forward(1, 1)
-    onward(1)
     b_forward(2)
     forward(0, 2)
     arrive(idw)
     idw = id_hop(3)
     forward(1, 2)
-    onward(2)
     b_forward(3)
-    arrive(cw[0], cw[1], by[0], by[1])
+    arrive(cw[0], cw[1], bx[0], bx[1])
+    for p in (0, 1):
+        spread(p)
     scores(known(0))
     forward(0, 3)
     arrive(idw)
     idw = id_hop(4)
     forward(1, 3)
-    b_forward(4)
-    arrive(cw[2], by[2])
+    arrive(cw[2], bx[2])
+    for p in (2, 3):
+        spread(p)
     scores(known(1))
     forward(0, 4)
     arrive(idw)
     arrive(cw[3], bx[3])
+    for p in (4, 5, 6):
+        spread(p)
     scores(known(2))
-    arrive(cw[4], bx[4])
-    last = known(3)
-    scores([t for t in last if t[:2] != (0, 3)])
+    scores([((1,), 3, gi) for gi in (0, 1, 2)])
+    arrive(cw[4])
+    scores([((1,), 3, 3)] + [(both, gt, 3) for gt in (0, 1, 2)])
     forward(1, 4)
-    scores([t for t in last if t[:2] == (0, 3)])
+    scores([((0,), 3, gi) for gi in (0, 1, 2, 3)])
 
     def image_part(gi):
         g = lax.dot_general(
             dst[:, gi * 256 : gi * 256 + 256], txt[...].reshape(1024, width),
             (((0,), (0,)), ((), ())), preferred_element_type=F32,
         ).reshape(2, 2, cap, width)
+        out = [None, None]
+        for k in (1, 0):
+            p, out[k] = 2 * gi + k, group()
+            gsend[p] = g[k, 1].astype(BF16)
+            send(gsend.at[p], grecv.at[p], core, out[k], 4)
         gown[2 * gi : 2 * gi + 2] = g[:, 0]
-        gsend[2 * gi : 2 * gi + 2] = g[:, 1].astype(BF16)
-        into, two = group(), pl.ds(2 * gi, 2)
-        send(gsend.at[two], grecv.at[two], core, into, 8)
-        return into
-
-    def text_part(half, gt):
+        return out
+
+    def text_part(gt):
         images = img[...].reshape(16 * cap, width)
-        t = jnp.dot(
-            dst[half * 512 + gt * 128 : half * 512 + gt * 128 + 128, :], images,
-            preferred_element_type=F32,
-        )
-        if half == 0:
-            for m in range(8):
-                ta[8 * gt + m] = pack(t[16 * m : 16 * m + 16])
-            return None
-        t = t.reshape(2, 4, 16, width)
+        d = jnp.concatenate([dst[at : at + 128, :] for at in (gt * 128, 512 + gt * 128)], axis=0)
+        t = jnp.dot(d, images, preferred_element_type=F32)
+        for m in range(8):
+            ta[8 * gt + m] = pack(t[16 * m : 16 * m + 16])
+        t = t[128:256].reshape(2, 4, 16, width)
         tb[2 * gt : 2 * gt + 2] = t[:, 0]
         bxs[2 * gt : 2 * gt + 2] = t[:, 1:].astype(BF16)
+
+    def text_across(gt):
         into, two = group(), pl.ds(2 * gt, 2)
         for k in (1, 2, 3):
             send(bxs.at[two, k - 1], bxr.at[two, k - 1], xk[k], into, 2)
@@ -416,33 +415,33 @@
     flows = ((image_sum, zs, zr_, (zp, zm)), (a_sum, as_, ar_, (yp, ym)))
     waits = {}
     cores, across = {}, {}
-    text_part(0, 3)
+    text_part(3)
     begin(1, 1)
+    across[3] = text_across(3)
     cores[3] = image_part(3)
-    across[3] = text_part(1, 3)
-    text_part(0, 2)
+    text_part(2)
     begin(1, 2)
+    across[2] = text_across(2)
     cores[2] = image_part(2)
-    arrive(cores[3])
+    arrive(cores[3][1])
     begin(0, 1)
-    across[2] = text_part(1, 2)
-    arrive(cores[2])
+    text_part(1)
+    across[1] = text_across(1)
+    arrive(cores[3][0], cores[2][1])
     begin(0, 2)
     carry(1, 2)
-    text_part(0, 1)
-    across[1] = text_part(1, 1)
     cores[1] = image_part(1)
     carry(0, 2)
-    text_part(0, 0)
-    across[0] = text_part(1, 0)
+    text_part(0)
+    across[0] = text_across(0)
     carry(1, 3)
-    arrive(cores[1])
+    arrive(cores[1][1], cores[2][0])
     cores[0] = image_part(0)
     carry(0, 3)
     arrive(across[3], across[2])
     far = b_far()
     carry(1, 4)
-    arrive(cores[0])
+    arrive(cores[0][1], cores[1][0])
     carry(0, 4)
     arrive(across[1], across[0], far)
     near = group()
@@ -461,6 +460,7 @@
         else:
             axs[q - 1] = value.astype(BF16)
             send(axs.at[q - 1], axr.at[q - 1], xk[q], axw, 1)
+    arrive(cores[0][0])
     total = jnp.concatenate([ring_total(0, q) for q in chunks])
     ig_ref[...] = jnp.where(live, unit_back(total, image_unit, image_inv), 0.0)
     arrive(axw)
@@ -484,7 +484,6 @@
     cap, width = tower_images.shape
     pairs = text.shape[0]
     vmem = pl.BlockSpec(memory_space=pltpu.VMEM)
-    smem = pl.BlockSpec(memory_space=pltpu.SMEM)
     V = pltpu.VMEM
     grads = pl.pallas_call(
         kernel,
@@ -492,7 +491,7 @@
             jax.ShapeDtypeStruct((cap, width), F32),
             jax.ShapeDtypeStruct((pairs, width), F32),
         ),
-        in_specs=[vmem, vmem, smem, vmem, smem, smem],
+        in_specs=[vmem] * 6,
         out_specs=(vmem, vmem),
         scratch_shapes=[
             V((8, 2, cap, width), BF16),
@@ -523,7 +522,10 @@
         compiler_params=pltpu.CompilerParams(
             collective_id=0, has_side_effects=True, vmem_limit_bytes=56 << 20
         ),
-    )(tower_images, owners.reshape(1, cap), counts, text, logit_scale, logit_bias)
+    )(
+        tower_images, owners.reshape(1, cap), counts.reshape(1, 1), text,
+        logit_scale.reshape(1, 1), logit_bias.reshape(1, 1),
+    )
     return pl.pallas_call(
         hand_out,
         out_shape=tuple(jax.ShapeDtypeStruct(g.shape, g.dtype) for g in grads),

time: 66.2 us -> 64.9 us (0.980)
  the two profiles are of different devices: /device:TPU:1 before, /device:TPU:24 now
where the time goes in v4:
time: 64.9 us; the launch traced here: 64.8 us
  Pallas kernels  62.2 us (96%)
  between operations  2.58 us (4%)
    pallas_call x1, Pallas kernels, shards(): pl.pallas_call(kernel, out_shape=(jax.ShapeDtypeStruct((cap, width), F32)...  60.4 us
    pallas_call x1, Pallas kernels, shards(): pl.pallas_call(hand_out, out_shape=tuple((jax.ShapeDtypeStruct(g.shape, g...  1.78 us

profile of v4, /device:TPU:24, one launch (start us, length us, event | category | flops | bytes accessed | tf_op | source)
XLA Modules:
  0.0 64.8 jit_solution(15751533933655853804)
XLA Ops:
  2.6 60.4 %shard_map.77 = (f32[64,1152]{1,0:T(8,128)}, f32[28,1152]{1,0:T(8,128)}) custom-call(bf16[64,1152]{1,0:T(8,128)(2,1)} %img_ref.1, s32[1,64]{1,0:T(1,128)} %bitcast.7, s32[1,1]{1,0:T(1,128)} %bitcast.4.cnt_ref, bf16[28,1152]{1,0:T(8,128)(2,1)} %text_ref.1, f32[1,1]{1,0:T(1,128)} %bitcast.5.scale_ref, f32[1,1]{1,0:T(1,128)} %bitcast.6.bias_ref), custom_call_target="tpu_custom_call" | custom-call | tf_op jit(solution)/shard_map/pallas_call | solution.py:488
  63.0 1.8 %shard_map.78 = (f32[64,1152]{1,0:T(8,128)}, f32[28,1152]{1,0:T(8,128)}) custom-call(f32[64,1152]{1,0:T(8,128)} %get-tuple-element.4.a_ref, f32[28,1152]{1,0:T(8,128)} %get-tuple-element.5.b_ref), custom_call_target="tpu_custom_call" | custom-call | tf_op jit(solution)/shard_map/pallas_call | solution.py:529

commit v5 on v4

--- a/solution.py
+++ b/solution.py
@@ -443,14 +443,6 @@
     carry(1, 4)
     arrive(cores[0][1], cores[1][0])
     carry(0, 4)
-    arrive(across[1], across[0], far)
-    near = group()
-    wide = came(1)
-    zeros = jnp.zeros((16, width), F32)
-    b_back(3, b_sum(pos(-2)) + came(0) + jnp.where(leftish, wide, zeros), ym2, near)
-    b_back(4, b_sum(pos(2)) + came(2) + jnp.where(leftish, zeros, wide), yp2, near)
-    b_back(5, b_sum(pos(-1)), ym, near)
-    b_back(6, b_sum(pos(1)), yp, near)
     axw = group(2)
     own_a = None
     for q in order:
@@ -461,6 +453,14 @@
             axs[q - 1] = value.astype(BF16)
             send(axs.at[q - 1], axr.at[q - 1], xk[q], axw, 1)
     arrive(cores[0][0])
+    arrive(across[1], across[0], far)
+    near = group()
+    wide = came(1)
+    zeros = jnp.zeros((16, width), F32)
+    b_back(3, b_sum(pos(-2)) + came(0) + jnp.where(leftish, wide, zeros), ym2, near)
+    b_back(4, b_sum(pos(2)) + came(2) + jnp.where(leftish, zeros, wide), yp2, near)
+    b_back(5, b_sum(pos(-1)), ym, near)
+    b_back(6, b_sum(pos(1)), yp, near)
     total = jnp.concatenate([ring_total(0, q) for q in chunks])
     ig_ref[...] = jnp.where(live, unit_back(total, image_unit, image_inv), 0.0)
     arrive(axw)
@@ -475,9 +475,24 @@
         wait(g, False)
 
 
-def hand_out(a_ref, b_ref, c_ref, d_ref):
-    c_ref[...] = a_ref[...]
-    d_ref[...] = b_ref[...]
+def hand_out(a_ref, b_ref, c_ref, d_ref, a_held, b_held, sems):
+    pieces = [(b_ref, b_held, d_ref)]
+    for first in range(0, a_ref.shape[0], 16):
+        rows = pl.ds(first, 16)
+        pieces.append((a_ref.at[rows], a_held.at[rows], c_ref.at[rows]))
+    into = [
+        pltpu.make_async_copy(src, held, sems.at[0, k]) for k, (src, held, _) in enumerate(pieces)
+    ]
+    out = [
+        pltpu.make_async_copy(held, to, sems.at[1, k]) for k, (_, held, to) in enumerate(pieces)
+    ]
+    for copy in into:
+        copy.start()
+    for arriving, leaving in zip(into, out):
+        arriving.wait()
+        leaving.start()
+    for copy in out:
+        copy.wait()
 
 
 def shards(tower_images, owners, counts, text, logit_scale, logit_bias):
@@ -526,11 +541,16 @@
         tower_images, owners.reshape(1, cap), counts.reshape(1, 1), text,
         logit_scale.reshape(1, 1), logit_bias.reshape(1, 1),
     )
+    anywhere = pl.BlockSpec(memory_space=pl.ANY)
     return pl.pallas_call(
         hand_out,
         out_shape=tuple(jax.ShapeDtypeStruct(g.shape, g.dtype) for g in grads),
-        in_specs=[vmem, vmem],
-        out_specs=(vmem, vmem),
+        in_specs=[anywhere, anywhere],
+        out_specs=(anywhere, anywhere),
+        scratch_shapes=[
+            V((cap, width), F32), V((pairs, width), F32),
+            pltpu.SemaphoreType.DMA((2, 1 + cap // 16)),
+        ],
     )(*grads)
 
 

time: 64.9 us -> 64.6 us (level)
  the two profiles are of different devices: /device:TPU:24 before, /device:TPU:1 now
where the time goes in v5:
time: 64.6 us; the launch traced here: 63.6 us
  Pallas kernels  61 us (94%)
  between operations  2.58 us (4%)
    pallas_call x1, Pallas kernels, shards(): pl.pallas_call(kernel, out_shape=(jax.ShapeDtypeStruct((cap, width), F32)...  59.2 us
    pallas_call x1, Pallas kernels, shards(): pl.pallas_call(hand_out, out_shape=tuple((jax.ShapeDtypeStruct(g.shape, g...  1.78 us

profile of v5, /device:TPU:1, one launch (start us, length us, event | category | flops | bytes accessed | tf_op | source)
XLA Modules:
  0.0 63.6 jit_solution(8258807479226103686)
XLA Ops:
  2.6 59.2 %shard_map.77 = (f32[64,1152]{1,0:T(8,128)}, f32[28,1152]{1,0:T(8,128)}) custom-call(bf16[64,1152]{1,0:T(8,128)(2,1)} %img_ref.1, s32[1,64]{1,0:T(1,128)} %bitcast.7, s32[1,1]{1,0:T(1,128)} %bitcast.4.cnt_ref, bf16[28,1152]{1,0:T(8,128)(2,1)} %text_ref.1, f32[1,1]{1,0:T(1,128)} %bitcast.5.scale_ref, f32[1,1]{1,0:T(1,128)} %bitcast.6.bias_ref), custom_call_target="tpu_custom_call" | custom-call | tf_op jit(solution)/shard_map/pallas_call | solution.py:503
  61.8 1.8 %shard_map.78 = (f32[64,1152]{1,0:T(8,128)}, f32[28,1152]{1,0:T(8,128)}) custom-call(f32[64,1152]{1,0:T(8,128)} %get-tuple-element.4.a_ref, f32[28,1152]{1,0:T(8,128)} %get-tuple-element.5.b_ref), custom_call_target="tpu_custom_call" | custom-call | tf_op jit(solution)/shard_map/pallas_call | solution.py:545
